TPU v7x, 32 devices: a whole 2x2x4 slice. The times are simulated.
32 devices in a mesh: dp: 8 (over z, core), node: 4 (over y, x).
Axes of the slice: x: 2, y: 2, z: 4, core: 2. Of those that a mesh axis runs over, the one named last changes fastest.
Arguments:
- inputs: bfloat16 [4096, 4096], P(('dp', 'node')), may hold values from -6 to 6
- queries: bfloat16 [4096, 4096], P(('dp', 'node')), may hold values from -130 to 130
- keys: bfloat16 [4096, 512], P(('dp', 'node')), may hold values from -6 to 6
- attention_gradient: bfloat16 [4096, 4096], P(('dp', 'node')), may hold values from -6 to 6
- value_matrix: bfloat16 [4096, 512], P('node'), may hold values from -0.09375 to 0.09375
Outputs:
- key_gradient: bfloat16 [4096, 512], P(('dp', 'node'))
- value_weight_gradient: float32 [4096, 512], P(('node', 'dp'))
All inputs are finite; a program needn't handle non-finite values.
Results may differ from a plain program's by a relative error of at most 0.009.
Values may be sent and summed in bfloat16 or wider, within the bound.
No kernel may reach another device: no remote copies, remote signals or barrier semaphores. Data moves between devices by JAX's collectives and lax.ppermute only.
A program may use at most 64 MiB of HBM per device.

v0:
```python
import jax
import jax.numpy as jnp
from jax import lax
from jax.sharding import PartitionSpec as P

QUERY_HEADS = 32
KEY_VALUE_HEADS = 4
HEAD_SIZE = 128


def attend(queries, keys, value_tensor, attention_gradient):
    sequence_length = queries.shape[0]
    group_count = QUERY_HEADS // KEY_VALUE_HEADS
    factor = HEAD_SIZE ** (-0.5)
    head_queries = queries.reshape(sequence_length, KEY_VALUE_HEADS, group_count, HEAD_SIZE)
    head_keys = keys.reshape(sequence_length, KEY_VALUE_HEADS, HEAD_SIZE)
    head_values = value_tensor.reshape(sequence_length, KEY_VALUE_HEADS, HEAD_SIZE)
    gradient_heads = attention_gradient.reshape(
        sequence_length, KEY_VALUE_HEADS, group_count, HEAD_SIZE
    )
    scores = (
        jnp.einsum("qhgd,khd->hgqk", head_queries, head_keys, preferred_element_type=jnp.float32)
        * factor
    )
    causal = jnp.arange(sequence_length)[:, None] >= jnp.arange(sequence_length)[None, :]
    scores = jnp.where(causal, scores, -1e30)
    largest = jnp.max(scores, axis=-1, keepdims=True)
    exponent = jnp.exp(scores - largest)
    attention = exponent / jnp.sum(exponent, axis=-1, keepdims=True)
    attention_low = attention.astype(jnp.bfloat16)
    d_attention = jnp.einsum(
        "qhgd,khd->hgqk", gradient_heads, head_values, preferred_element_type=jnp.float32
    )
    row_dots = jnp.sum(attention * d_attention, axis=-1, keepdims=True)
    d_scores = (attention * (d_attention - row_dots)).astype(jnp.bfloat16)
    key_gradient = (
        jnp.einsum("hgqk,qhgd->khd", d_scores, head_queries, preferred_element_type=jnp.float32)
        * factor
    ).astype(jnp.bfloat16)
    value_gradient = jnp.einsum(
        "hgqk,qhgd->khd", attention_low, gradient_heads, preferred_element_type=jnp.float32
    ).astype(jnp.bfloat16)
    return (
        key_gradient.reshape(sequence_length, KEY_VALUE_HEADS * HEAD_SIZE),
        value_gradient.reshape(sequence_length, KEY_VALUE_HEADS * HEAD_SIZE),
    )


def add_rows(source, portion):
    return jnp.dot(source, portion, preferred_element_type=jnp.float32)


def per_device(inputs, queries, keys, attention_gradient, value_matrix):
    devices = lax.axis_size("dp") * lax.axis_size("node")
    value_tensor = add_rows(
        inputs, lax.all_gather(value_matrix, "node", axis=0, tiled=True)
    ).astype(jnp.bfloat16)
    key_gradient, value_gradient = attend(queries, keys, value_tensor, attention_gradient)
    local_grad = lax.dot_general(
        inputs, value_gradient, (((0,), (0,)), ((), ())), preferred_element_type=jnp.float32
    )
    node_sum = lax.psum_scatter(
        local_grad.astype(jnp.bfloat16), "node", scatter_dimension=0, tiled=True
    ).astype(jnp.float32)
    owned = lax.psum_scatter(node_sum, "dp", scatter_dimension=0, tiled=True)
    return (key_gradient, owned / devices)


def solution(mesh):
    placed = (
        P(("dp", "node"), None),
        P(("dp", "node"), None),
        P(("dp", "node"), None),
        P(("dp", "node"), None),
        P("node", None),
    )
    return jax.shard_map(
        per_device,
        mesh=mesh,
        in_specs=placed,
        out_specs=(P(("dp", "node"), None), P(("node", "dp"), None)),
        check_vma=False,
    )
```

profile of v0, /device:TPU:0, one launch (start us, length us, event | category | flops | bytes accessed | tf_op | source)
XLA Modules:
  0.0 175.7 jit_solution(10382161808785498208)
XLA Ops:
  7.2 0.0 copy-start
  7.2 0.0 reduce-scatter.3.cloned.1.call-start
  7.3 1.1 reshape.25
  8.3 1.6 copy.27
  10.0 1.3 copy.28
  11.3 2.2 %fusion.27 = (f32[4,8,128]{2,1,0:T(8,128)S(1)}, f32[4,8,128,128]{2,3,1,0:T(8,128)}) fusion(pred[128,128]{0,1:T(8,128)(4,1)S(1)} %iota_compare_fusion, bf16[128,4,8,128]{0,3,2,1:T(8,128)(2,1)S(1)} %bitcast.49, bf16[128,4,128,1]{2,1,0,3:T(4,128)(2,1)S(1)} %bitcast.54), kind=kOutput, calls=%fused_computation.31 | convolution fusion | flops 136315008 | bytes 3309568 | tf_op jit(solution)/shard_map/sub | solution.py:28
  13.5 2.0 %fusion.8 = bf16[4,128,128]{1,2,0:T(8,128)(2,1)S(1)} fusion(bf16[128,4,8,128]{0,3,2,1:T(8,128)(2,1)S(1)} %bitcast.51, f32[4,8,128,128]{2,3,1,0:T(8,128)} %get-tuple-element.5, f32[4,8,128]{2,1,0:T(8,128)S(1)} %get-tuple-element.4), kind=kOutput, calls=%fused_computation.16 | convolution fusion | flops 135331840 | bytes 3293184 | tf_op jit(solution)/shard_map/hgqk,qhgd->khd/dot_general | solution.py:40
  15.5 3.2 %fusion.1 = bf16[4096,512]{0,1:T(8,128)(2,1)} fusion(bf16[128,512]{0,1:T(8,128)(2,1)S(1)} %bitcast.53, bf16[128,4096]{1,0:T(8,128)(2,1)S(1)} %copy-done), kind=kOutput, calls=%fused_computation.2 | convolution fusion | flops 538968064 | bytes 5373952 | tf_op jit(solution)/shard_map/dot_general | solution.py:59
  18.8 0.0 reduce-scatter.3.cloned.1.call-update
  18.8 0.0 all-gather.2.cloned.1.call-start
  18.8 0.7 all-gather.2.cloned.1.call-update
  19.5 0.0 reduce-scatter.5.cloned.1.call-start
  19.6 54.7 %reduce-scatter.3.cloned.1.call-done = bf16[1024,512]{0,1:T(8,128)(2,1)} async-done(((bf16[4096,512]{0,1:T(8,128)(2,1)}), bf16[1024,512]{0,1:T(8,128)(2,1)}) %reduce-scatter.3.cloned.1.call-update) | async-done | bytes 1048592 | tf_op jit(solution)/shard_map/reduce_scatter | solution.py:62
  74.3 2.8 %convert_element_type.39 = f32[1024,512]{0,1:T(8,128)} convert(bf16[1024,512]{0,1:T(8,128)(2,1)} %reduce-scatter.3.cloned.1.call-done) | non-fusion elementwise | flops 524288 | bytes 3145728 | tf_op jit(solution)/shard_map/convert_element_type | solution.py:64
  77.1 0.0 reduce-scatter.5.cloned.1.call-update
  77.1 51.9 %all-gather.2.cloned.1.call-done = bf16[4096,512]{1,0:T(8,128)(2,1)} async-done(((bf16[1024,512]{1,0:T(8,128)(2,1)}), bf16[4096,512]{1,0:T(8,128)(2,1)}) %all-gather.2.cloned.1.call-update) | async-done | bytes 4194320 | tf_op jit(solution)/shard_map/all_gather | solution.py:56
  129.0 2.9 %convolution_convert_fusion.1 = bf16[128,512]{1,0:T(8,128)(2,1)S(1)} fusion(bf16[128,4096]{1,0:T(8,128)(2,1)S(1)} %copy-done, bf16[4096,512]{1,0:T(8,128)(2,1)} %all-gather.2.cloned.1.call-done), kind=kOutput, calls=%fused_computation.15 | convolution fusion | flops 536936448 | bytes 5373952 | tf_op jit(solution)/shard_map/dot_general | solution.py:50
  132.0 2.2 %fusion.2 = (f32[4,8,128]{2,1,0:T(8,128)S(1)}, f32[4,128,128,8]{2,1,3,0:T(8,128)S(1)}) fusion(f32[4,8,128,128]{2,3,1,0:T(8,128)} %get-tuple-element.5, f32[4,8,128]{2,1,0:T(8,128)S(1)} %get-tuple-element.4, bf16[128,4,8,128]{0,3,2,1:T(8,128)(2,1)S(1)} %bitcast.52, bf16[128,4,128,1]{2,1,0,3:T(4,128)(2,1)S(1)} %bitcast.56), kind=kOutput, calls=%fused_computation.5 | convolution fusion | flops 135786496 | bytes 5406720 | tf_op jit(solution)/shard_map/qhgd,khd->hgqk/dot_general | solution.py:31
  134.2 0.0 copy-done.3
  134.2 0.5 fusion.7
  134.7 0.8 copy.15
  135.5 31.8 %reduce-scatter.5.cloned.1.call-done = f32[128,512]{0,1:T(8,128)} async-done(((f32[1024,512]{0,1:T(8,128)}), f32[128,512]{0,1:T(8,128)}) %reduce-scatter.5.cloned.1.call-update) | async-done | bytes 262160 | tf_op jit(solution)/shard_map/reduce_scatter | solution.py:65
  167.3 1.0 broadcast_multiply_fusion
  168.3 0.8 copy.16
  (8 shorter events, 0.1 us)
Async XLA Ops:
  7.2 8.4 %copy-start = (bf16[128,4096]{1,0:T(8,128)(2,1)S(1)}, bf16[128,4096]{1,0:T(8,128)(2,1)}, u32[]{:S(2)}) copy-start(bf16[128,4096]{1,0:T(8,128)(2,1)} %param.5) | copy-start | bytes 3145732
  7.2 2.8 %copy-start.1 = (bf16[128,4096]{1,0:T(8,128)(2,1)S(1)}, bf16[128,4096]{1,0:T(8,128)(2,1)}, u32[]{:S(2)}) copy-start(bf16[128,4096]{1,0:T(8,128)(2,1)} %param.8) | copy-start | bytes 3145732
  7.2 67.1 %reduce-scatter.3.cloned.1.call-start = ((), (), s32[]{:S(2)}) async-start(), calls=%async_computation.3 | async-start | bytes 5242880 | tf_op jit(solution)/shard_map/reduce_scatter | solution.py:62
  11.3 2.2 %copy-start.2 = (bf16[128,4096]{0,1:T(8,128)(2,1)S(1)}, bf16[128,4096]{0,1:T(8,128)(2,1)}, u32[]{:S(2)}) copy-start(bf16[128,4096]{0,1:T(8,128)(2,1)} %copy.28) | copy-start | bytes 3145732
  18.8 110.2 %all-gather.2.cloned.1.call-start = ((), (), s32[]{:S(2)}) async-start(), calls=%async_computation.2 | async-start | bytes 5242880 | tf_op jit(solution)/shard_map/all_gather | solution.py:56
  19.5 147.8 %reduce-scatter.5.cloned.1.call-start = ((), (), s32[]{:S(2)}) async-start(), calls=%async_computation.4 | async-start | bytes 2359296 | tf_op jit(solution)/shard_map/reduce_scatter | solution.py:65
  132.0 2.2 %copy-start.3 = (f32[4,8,128,128]{2,3,1,0:T(8,128)S(1)}, f32[4,8,128,128]{2,3,1,0:T(8,128)}, u32[]{:S(2)}) copy-start(f32[4,8,128,128]{2,3,1,0:T(8,128)} %get-tuple-element.5) | copy-start | bytes 6291460
Sparse Core Ops, SparseCore 0:
  18.9 55.3 reduce-scatter.2
  76.3 52.6 all-gather.1
  131.4 35.8 reduce-scatter.4
where the time goes:
time: 176 us
  waiting for transfers between devices  139 us (79%)
  between operations  13.8 us (8%)
  matrix products  13.1 us (7%)
  local copies, waits for them, and re-layouts  5.71 us (3%)
  other arithmetic  3.78 us (2%)
    reduce_scatter x1, waiting for transfers between devices, per_device(): lax.psum_scatter(local_grad.astype(jnp.bfloat16), 'node', scatter_dimensi...  54.7 us
    all_gather x1, waiting for transfers between devices, per_device(): lax.all_gather(value_matrix, 'node', axis=0, tiled=True)  51.9 us
    reduce_scatter x1, waiting for transfers between devices, per_device(): owned = lax.psum_scatter(node_sum, 'dp', scatter_dimension=0, tiled=True)  31.8 us
  transfers between devices with their start and end apart: 3, of which 3 were waited for; matrix products, arithmetic and copies ran while one was open for 5% of the time, Pallas kernels for 0%

commit v1 on v0

v1 whole, which is shorter than its diff:
```python
import functools

import jax
import jax.numpy as jnp
from jax import lax
from jax.experimental import pallas as pl
from jax.experimental.pallas import tpu as pltpu
from jax.sharding import PartitionSpec as P

QUERY_HEADS = 32
KEY_VALUE_HEADS = 4
HEAD_SIZE = 128
GROUP = QUERY_HEADS // KEY_VALUE_HEADS
FACTOR = HEAD_SIZE ** (-0.5)
LOG2_E = 1.4426950408889634
VMEM = pl.BlockSpec(memory_space=pltpu.VMEM)


def dot(a, b):
    return jnp.dot(a, b, preferred_element_type=jnp.float32)


def dot_nt(a, b):
    return lax.dot_general(a, b, (((1,), (1,)), ((), ())), preferred_element_type=jnp.float32)


def dot_tn(a, b):
    return lax.dot_general(a, b, (((0,), (0,)), ((), ())), preferred_element_type=jnp.float32)


def head(ref, h):
    return ref[:, h * HEAD_SIZE : (h + 1) * HEAD_SIZE]


def softmax_kernel(q_ref, k_ref, g_ref, dv_ref, p_ref):
    tokens = q_ref.shape[0]
    key = k_ref[...]
    seen = lax.broadcasted_iota(jnp.int32, (tokens, tokens), 0) <= lax.broadcasted_iota(
        jnp.int32, (tokens, tokens), 1
    )
    total = None
    for h in range(GROUP):
        scores = jnp.where(seen, dot_nt(key, head(q_ref, h)), -1e30)
        exponent = jnp.exp2((scores - jnp.max(scores, axis=0, keepdims=True)) * (FACTOR * LOG2_E))
        attention = exponent * (1.0 / jnp.sum(exponent, axis=0, keepdims=True))
        p_ref[:, h * tokens : (h + 1) * tokens] = attention
        part = dot(attention.astype(jnp.bfloat16), head(g_ref, h))
        total = part if total is None else total + part
    dv_ref[...] = total.astype(jnp.bfloat16)


def softmax_call(queries, keys, gradient):
    tokens = queries.shape[0]
    wide = pl.BlockSpec((tokens, GROUP * HEAD_SIZE), lambda g: (0, g))
    narrow = pl.BlockSpec((tokens, HEAD_SIZE), lambda g: (0, g))
    return pl.pallas_call(
        softmax_kernel,
        grid=(KEY_VALUE_HEADS,),
        in_specs=[wide, narrow, wide],
        out_specs=[narrow, pl.BlockSpec((tokens, GROUP * tokens), lambda g: (0, g))],
        out_shape=[
            jax.ShapeDtypeStruct((tokens, KEY_VALUE_HEADS * HEAD_SIZE), jnp.bfloat16),
            jax.ShapeDtypeStruct((tokens, QUERY_HEADS * tokens), jnp.float32),
        ],
        cost_estimate=pl.CostEstimate(flops=4_000_000_000, bytes_accessed=8_000_000, transcendentals=0),
    )(queries, keys, gradient)


def key_kernel(q_ref, g_ref, p_ref, *rest):
    value_refs, out_ref = rest[:-1], rest[-1]
    tokens = q_ref.shape[0]
    value = value_refs[0][...].astype(jnp.float32)
    for ref in value_refs[1:]:
        value = value + ref[...].astype(jnp.float32)
    value = value.astype(jnp.bfloat16)
    total = None
    for h in range(GROUP):
        attention = p_ref[:, h * tokens : (h + 1) * tokens]
        d_attention = dot_nt(value, head(g_ref, h))
        row_dots = jnp.sum(attention * d_attention, axis=0, keepdims=True)
        d_scores = (attention * (d_attention - row_dots)).astype(jnp.bfloat16)
        part = dot(d_scores, head(q_ref, h))
        total = part if total is None else total + part
    out_ref[...] = (total * FACTOR).astype(jnp.bfloat16)


def key_call(queries, gradient, attention, values):
    tokens = queries.shape[0]
    wide = pl.BlockSpec((tokens, GROUP * HEAD_SIZE), lambda g: (0, g))
    narrow = pl.BlockSpec((tokens, HEAD_SIZE), lambda g: (0, g))
    return pl.pallas_call(
        key_kernel,
        grid=(KEY_VALUE_HEADS,),
        in_specs=[wide, wide, pl.BlockSpec((tokens, GROUP * tokens), lambda g: (0, g))] + [narrow] * len(values),
        out_specs=narrow,
        out_shape=jax.ShapeDtypeStruct((tokens, KEY_VALUE_HEADS * HEAD_SIZE), jnp.bfloat16),
        cost_estimate=pl.CostEstimate(flops=4_000_000_000, bytes_accessed=8_000_000, transcendentals=0),
    )(queries, gradient, attention, *values)


def values_kernel(*refs):
    n = len(refs) // 2
    weights = refs[n][...]
    for source, out in zip(refs[:n], refs[n + 1 :]):
        out[...] = dot(source[...], weights).astype(out.dtype)


def values_call(blocks, weights):
    n = len(blocks)
    shape = (blocks[0].shape[0], weights.shape[1])
    return pl.pallas_call(
        values_kernel,
        in_specs=[VMEM] * (n + 1),
        out_specs=[VMEM] * n,
        out_shape=[jax.ShapeDtypeStruct(shape, jnp.float32 if i == 0 else jnp.bfloat16) for i in range(n)],
        cost_estimate=pl.CostEstimate(flops=2_000_000_000, bytes_accessed=3_000_000, transcendentals=0),
    )(*blocks, weights)


def weight_kernel(n, place_ref, *refs):
    blocks, d_values, send_ref, keep_ref = refs[:n], refs[n : 2 * n], refs[2 * n], refs[2 * n + 1]
    rows = keep_ref.shape[1]
    core = place_ref[0]
    values = jnp.concatenate([ref[...] for ref in d_values], axis=0)
    for i in range(keep_ref.shape[0]):
        for parity, out in ((1 - core, send_ref), (core, keep_ref)):
            columns = pl.ds(pl.multiple_of((2 * i + parity) * rows, rows), rows)
            source = jnp.concatenate([ref[:, columns] for ref in blocks], axis=0)
            out[i] = dot_tn(source, values).astype(out.dtype)


def weight_call(blocks, d_values, core, owners):
    n = len(blocks)
    width = d_values[0].shape[1]
    shape = (owners // 2, blocks[0].shape[1] // owners, width)
    return pl.pallas_call(
        functools.partial(weight_kernel, n),
        in_specs=[pl.BlockSpec(memory_space=pltpu.SMEM)] + [VMEM] * (2 * n),
        out_specs=[VMEM] * 2,
        out_shape=[jax.ShapeDtypeStruct(shape, jnp.bfloat16), jax.ShapeDtypeStruct(shape, jnp.float32)],
        cost_estimate=pl.CostEstimate(flops=2_000_000_000, bytes_accessed=3_000_000, transcendentals=0),
    )(core.reshape(1), *blocks, *d_values)


def swap(array, axis, distance):
    size = lax.axis_size(axis)
    return lax.ppermute(array, axis, [(i, i ^ distance) for i in range(size)])


def per_device(inputs, queries, keys, attention_gradient, value_matrix):
    nodes, owners = lax.axis_size("node"), lax.axis_size("dp")
    node, owner = lax.axis_index("node"), lax.axis_index("dp")
    width = inputs.shape[1] // nodes

    def columns_of(other):
        return lax.dynamic_slice_in_dim(inputs, other * width, width, axis=1)

    blocks = [columns_of(node)]
    blocks += [swap(columns_of(node ^ k), "node", k) for k in range(1, nodes)]
    d_values, attention = softmax_call(queries, keys, attention_gradient)
    all_d_values = [d_values] + [swap(d_values, "node", k) for k in range(1, nodes)]
    parts = values_call(blocks, value_matrix)
    values = [parts[0]] + [swap(parts[k], "node", k) for k in range(1, nodes)]
    key_gradient = key_call(queries, attention_gradient, attention, values)

    rows = width // owners
    if rows % 16 or owners % 2:
        local = dot_tn(jnp.concatenate(blocks, axis=0), jnp.concatenate(all_d_values, axis=0))
        owned = lax.psum_scatter(local, "dp", scatter_dimension=0, tiled=True)
        return key_gradient, owned / (owners * nodes)
    core, chip, chips = owner % 2, owner // 2, owners // 2
    send, keep = weight_call(blocks, all_d_values, core, owners)
    pair = keep + swap(send, "dp", 1).astype(jnp.float32)

    def chip_rows(other):
        return lax.dynamic_index_in_dim(pair, other, axis=0, keepdims=False)

    owned = chip_rows(chip)
    for k in range(1, chips):
        owned += swap(chip_rows(chip ^ k).astype(jnp.bfloat16), "dp", 2 * k).astype(jnp.float32)
    return key_gradient, owned / (owners * nodes)


def solution(mesh):
    placed = (
        P(("dp", "node"), None),
        P(("dp", "node"), None),
        P(("dp", "node"), None),
        P(("dp", "node"), None),
        P("node", None),
    )
    return jax.shard_map(
        per_device,
        mesh=mesh,
        in_specs=placed,
        out_specs=(P(("dp", "node"), None), P(("node", "dp"), None)),
        check_vma=False,
    )
```

time: 176 us -> 55.3 us (0.31)
  waiting for transfers between devices: 139 us -> 16 us
  starting transfers between devices: 0.12 us -> 18.5 us
  Pallas kernels: 0 us -> 16.4 us
  matrix products: 13.1 us -> 0 us
  between operations: 13.8 us -> 0.72 us
  local copies, waits for them, and re-layouts: 5.71 us -> 2.42 us
  other arithmetic: 3.78 us -> 0.94 us
    reduce_scatter x2 -> x0, waiting for transfers between devices: 86.5 us -> none  [the longest x1 54.7 us: per_device(): lax.psum_scatter(local_grad.astype(jnp.bfloat16), 'node', scatter_dimensi...]
    all_gather x1 -> x0, waiting for transfers between devices: 51.9 us -> none  [per_device(): lax.all_gather(value_matrix, 'node', axis=0, tiled=True)]
    ppermute x0 -> x13, starting transfers between devices: none -> 18.5 us  [swap(): return lax.ppermute(array, axis, [(i, i ^ distance) for i in range(size)])]
    pallas_call x0 -> x4, Pallas kernels: none -> 16.4 us  [the longest x1 5.15 us: key_call(): pl.pallas_call(key_kernel, grid=(KEY_VALUE_HEADS,), in_specs=[wide, wide,...]
    ppermute x0 -> x13, waiting for transfers between devices: none -> 16 us  [swap(): return lax.ppermute(array, axis, [(i, i ^ distance) for i in range(size)])]
    dot_general x5 -> x0, matrix products: 10.9 us -> none  [the longest x1 3.21 us: per_device(): lax.dot_general(inputs, value_gradient, (((0,), (0,)), ((), ())), preferr...]
    reshape x4 -> x0, local copies, waits for them, and re-layouts: 4.05 us -> none  [the longest x1 1.62 us: attend(): queries.reshape(sequence_length, KEY_VALUE_HEADS, group_count, HEAD_SIZE)]
    convert_element_type x1 -> x0, other arithmetic: 2.79 us -> none  [per_device(): node_sum = lax.psum_scatter(local_grad.astype(jnp.bfloat16), 'node', scat...]
  transfers between devices with their start and end apart: 3 -> 13, of which waited for: 3 -> 4; matrix products, arithmetic and copies ran while one was open for 5% -> 2% of each run, Pallas kernels for 0% -> 15%
where the time goes in v1:
time: 55.3 us; the launch traced here: 55 us
  starting transfers between devices  18.5 us (33%)
  Pallas kernels  16.4 us (30%)
  waiting for transfers between devices  16 us (29%)
  local copies, waits for them, and re-layouts  2.42 us (4%)
  other arithmetic  0.94 us (2%)
  between operations  0.72 us (1%)
    ppermute x13, starting transfers between devices, swap(): return lax.ppermute(array, axis, [(i, i ^ distance) for i in range(size)])  18.5 us
    ppermute x13, waiting for transfers between devices, swap(): return lax.ppermute(array, axis, [(i, i ^ distance) for i in range(size)])  16 us
    pallas_call x1, Pallas kernels, key_call(): pl.pallas_call(key_kernel, grid=(KEY_VALUE_HEADS,), in_specs=[wide, wide,...  5.15 us
    pallas_call x1, Pallas kernels, softmax_call(): pl.pallas_call(softmax_kernel, grid=(KEY_VALUE_HEADS,), in_specs=[wide, n...  5.07 us
    pallas_call x1, Pallas kernels, weight_call(): pl.pallas_call(functools.partial(weight_kernel, n), in_specs=[pl.BlockSpe...  3.19 us
    pallas_call x1, Pallas kernels, values_call(): pl.pallas_call(values_kernel, in_specs=[VMEM] * (n + 1), out_specs=[VMEM]...  3.02 us
    unnamed x24, local copies, waits for them, and re-layouts  1.57 us
  transfers between devices with their start and end apart: 13, of which 4 were waited for; matrix products, arithmetic and copies ran while one was open for 2% of the time, Pallas kernels for 15%

profile of v1, /device:TPU:0, one launch (start us, length us, event | category | flops | bytes accessed | tf_op | source)
XLA Modules:
  0.0 55.0 jit_solution(6870611735985800342)
XLA Ops:
  0.6 5.1 %shard_map.68 = (bf16[128,512]{1,0:T(8,128)(2,1)}, f32[128,4096]{1,0:T(8,128)}) custom-call(bf16[128,4096]{1,0:T(8,128)(2,1)} %q_ref.3, bf16[128,512]{1,0:T(8,128)(2,1)} %k_ref.1, bf16[128,4096]{1,0:T(8,128)(2,1)} %g_ref.3), custom_call_target="tpu_custom_call" | custom-call | flops 4000000000 | bytes 8000000 | tf_op jit(solution)/shard_map/pallas_call | solution.py:56
  5.7 3.9 %collective-permute-start.8 = (bf16[128,512]{1,0:T(8,128)(2,1)}, bf16[128,512]{1,0:T(8,128)(2,1)S(1)}, u32[]{:S(2)}, u32[]{:S(2)}) collective-permute-start(bf16[128,512]{1,0:T(8,128)(2,1)} %get-tuple-element.15.refs_4_), channel_id=1, source_target_pairs={{0,3},{1,2},{2,1},{3,0},{4,7},{5,6},{6,5},{7,4},{8,11},{9,10},{10,... | collective-permute-start | bytes 393224 | tf_op jit(solution)/shard_map/ppermute | solution.py:147
  9.6 0.8 %constant_dynamic-slice_fusion = (bf16[128,1024]{1,0:T(8,128)(2,1)S(1)}, bf16[128,1024]{1,0:T(8,128)(2,1)S(1)}, bf16[128,1024]{1,0:T(8,128)(2,1)}, bf16[128,1024]{1,0:T(8,128)(2,1)S(1)}) fusion(bf16[128,4096]{1,0:T(8,128)(2,1)S(1)} %copy-done, s32[]{:T(128)S(6)} %select_n.39, s32[]{:T(128)S(6)} %select_n.37, s32[]{:T(128)S(6)} %select_n.36, s32[]{:T(128)S(6)} %select_n.38), kind=kLoop, calls=%fused_computation.11 | loop fusion | bytes 2097168 | tf_op jit(solution)/shard_map/dynamic_slice | solution.py:156
  10.5 1.9 %collective-permute-start = (bf16[128,1024]{1,0:T(8,128)(2,1)S(1)}, bf16[128,1024]{1,0:T(8,128)(2,1)S(1)}, u32[]{:S(2)}, u32[]{:S(2)}) collective-permute-start(bf16[128,1024]{1,0:T(8,128)(2,1)S(1)} %get-tuple-element.22), channel_id=1, source_target_pairs={{0,1},{1,0},{2,3},{3,2},{4,5},{5,4},{6,7},{7,6},{8,9},{9,8},{10,11... | collective-permute-start | bytes 786440 | tf_op jit(solution)/shard_map/ppermute | solution.py:147
  12.4 1.5 %collective-permute-start.1 = (bf16[128,1024]{1,0:T(8,128)(2,1)S(1)}, bf16[128,1024]{1,0:T(8,128)(2,1)S(1)}, u32[]{:S(2)}, u32[]{:S(2)}) collective-permute-start(bf16[128,1024]{1,0:T(8,128)(2,1)S(1)} %get-tuple-element.24), channel_id=1, source_target_pairs={{0,2},{1,3},{2,0},{3,1},{4,6},{5,7},{6,4},{7,5},{8,10},{9,11},{10,... | collective-permute-start | bytes 786440 | tf_op jit(solution)/shard_map/ppermute | solution.py:147
  13.9 0.5 collective-permute-start.7
  14.4 1.7 %collective-permute-start.6 = (bf16[128,512]{1,0:T(8,128)(2,1)S(1)}, bf16[128,512]{1,0:T(8,128)(2,1)S(1)}, u32[]{:S(2)}, u32[]{:S(2)}) collective-permute-start(bf16[128,512]{1,0:T(8,128)(2,1)S(1)} %copy-done.5), channel_id=1, source_target_pairs={{0,1},{1,0},{2,3},{3,2},{4,5},{5,4},{6,7},{7,6},{8,9},{9,8},{10,11... | collective-permute-start | bytes 393224 | tf_op jit(solution)/shard_map/ppermute | solution.py:147
  16.1 11.4 %collective-permute-done.7.refs_6_ = bf16[128,512]{1,0:T(8,128)(2,1)S(1)} collective-permute-done((bf16[128,512]{1,0:T(8,128)(2,1)S(1)}, bf16[128,512]{1,0:T(8,128)(2,1)S(1)}, u32[]{:S(2)}, u32[]{:S(2)}) %collective-permute-start.7) | collective-permute-done | bytes 131104 | tf_op jit(solution)/shard_map/ppermute | solution.py:147
  27.7 0.4 copy-done.7
  28.1 0.2 copy-done.9
  28.6 3.2 %shard_map.71 = (bf16[4,128,512]{2,1,0:T(8,128)(2,1)}, f32[4,128,512]{2,1,0:T(8,128)}) custom-call(s32[1]{0:T(128)} %bitcast.place_ref, bf16[128,1024]{1,0:T(8,128)(2,1)} %get-tuple-element.23.refs_0_, bf16[128,1024]{1,0:T(8,128)(2,1)} %copy-done.3, bf16[128,1024]{1,0:T(8,128)(2,1)} %copy-done.4, bf16[128,1024]{1,0:T(8,128)(2,1)} %copy-done.2, ...), custom_call_target="tpu_custom_call" | custom-call | flops 2000000000 | bytes 3000000 | tf_op jit(solution)/shard_map/pallas_call | solution.py:136
  31.8 3.0 %shard_map.69 = (f32[128,512]{1,0:T(8,128)}, bf16[128,512]{1,0:T(8,128)(2,1)}, bf16[128,512]{1,0:T(8,128)(2,1)}, bf16[128,512]{1,0:T(8,128)(2,1)}) custom-call(bf16[128,1024]{1,0:T(8,128)(2,1)} %get-tuple-element.23.refs_0_, bf16[128,1024]{1,0:T(8,128)(2,1)} %copy-done.3, bf16[128,1024]{1,0:T(8,128)(2,1)} %copy-done.4, bf16[128,1024]{1,0:T(8,128)(2,1)} %copy-done.2, ...), custom_call_target="tpu_custom_call" | custom-call | flops 2000000000 | bytes 3000000 | tf_op jit(solution)/shard_map/pallas_call | solution.py:111
  34.8 1.5 %collective-permute-start.3 = (bf16[128,512]{1,0:T(8,128)(2,1)}, bf16[128,512]{1,0:T(8,128)(2,1)S(1)}, u32[]{:S(2)}, u32[]{:S(2)}) collective-permute-start(bf16[128,512]{1,0:T(8,128)(2,1)} %get-tuple-element.12), channel_id=1, source_target_pairs={{0,1},{1,0},{2,3},{3,2},{4,5},{5,4},{6,7},{7,6},{8,9},{9,8},{10,11... | collective-permute-start | bytes 393224 | tf_op jit(solution)/shard_map/ppermute | solution.py:147
  36.3 1.5 %collective-permute-start.4 = (bf16[128,512]{1,0:T(8,128)(2,1)}, bf16[128,512]{1,0:T(8,128)(2,1)S(1)}, u32[]{:S(2)}, u32[]{:S(2)}) collective-permute-start(bf16[128,512]{1,0:T(8,128)(2,1)} %get-tuple-element.13), channel_id=1, source_target_pairs={{0,2},{1,3},{2,0},{3,1},{4,6},{5,7},{6,4},{7,5},{8,10},{9,11},{10,... | collective-permute-start | bytes 393224 | tf_op jit(solution)/shard_map/ppermute | solution.py:147
  37.8 0.5 collective-permute-start.5
  38.3 0.2 convert_add_fusion
  38.5 1.6 %collective-permute-start.10 = (bf16[128,512]{1,0:T(8,128)(2,1)S(1)}, bf16[128,512]{1,0:T(8,128)(2,1)S(1)}, u32[]{:S(2)}, u32[]{:S(2)}) collective-permute-start(bf16[128,512]{1,0:T(8,128)(2,1)S(1)} %get-tuple-element.18), channel_id=1, source_target_pairs={{0,8},{4,12},{8,0},{12,4},{16,24},{20,28},{24,16},{28,20},{1,9},{5... | collective-permute-start | bytes 393224 | tf_op jit(solution)/shard_map/ppermute | solution.py:147
  40.2 2.5 %collective-permute-start.12 = (bf16[128,512]{1,0:T(8,128)(2,1)S(1)}, bf16[128,512]{1,0:T(8,128)(2,1)S(1)}, u32[]{:S(2)}, u32[]{:S(2)}) collective-permute-start(bf16[128,512]{1,0:T(8,128)(2,1)S(1)} %get-tuple-element.19), channel_id=1, source_target_pairs={{0,24},{4,28},{8,16},{12,20},{16,8},{20,12},{24,0},{28,4},{1,25},{... | collective-permute-start | bytes 393224 | tf_op jit(solution)/shard_map/ppermute | solution.py:147
  42.7 1.2 %collective-permute-start.11 = (bf16[128,512]{1,0:T(8,128)(2,1)S(1)}, bf16[128,512]{1,0:T(8,128)(2,1)S(1)}, u32[]{:S(2)}, u32[]{:S(2)}) collective-permute-start(bf16[128,512]{1,0:T(8,128)(2,1)S(1)} %get-tuple-element.20), channel_id=1, source_target_pairs={{0,16},{4,20},{8,24},{12,28},{16,0},{20,4},{24,8},{28,12},{1,17},{... | collective-permute-start | bytes 393224 | tf_op jit(solution)/shard_map/ppermute | solution.py:147
  43.9 1.0 %collective-permute-done.4.rest_2_ = bf16[128,512]{1,0:T(8,128)(2,1)S(1)} collective-permute-done((bf16[128,512]{1,0:T(8,128)(2,1)}, bf16[128,512]{1,0:T(8,128)(2,1)S(1)}, u32[]{:S(2)}, u32[]{:S(2)}) %collective-permute-start.4) | collective-permute-done | bytes 131104 | tf_op jit(solution)/shard_map/ppermute | solution.py:147
  44.9 0.6 %copy-done.10 = bf16[128,512]{1,0:T(8,128)(2,1)} copy-done((bf16[128,512]{1,0:T(8,128)(2,1)}, bf16[128,512]{1,0:T(8,128)(2,1)S(1)}, u32[]{:S(2)}) %copy-start.10) | copy-done | bytes 131096
  45.6 5.2 %shard_map.70 = bf16[128,512]{1,0:T(8,128)(2,1)} custom-call(bf16[128,4096]{1,0:T(8,128)(2,1)} %q_ref.3, bf16[128,4096]{1,0:T(8,128)(2,1)} %g_ref.3, f32[128,4096]{1,0:T(8,128)} %get-tuple-element.10.p_ref, f32[128,512]{1,0:T(8,128)} %get-tuple-element.11.rest_0_, bf16[128,512]{1,0:T(8,128)(2,1)} %copy-done.8, bf16[128,512]{1,0:T(8,128)(2,1)} %copy-done.10, ...), custom_call_target="tpu_custom_call" | custom-call | flops 4000000000 | bytes 8000000 | tf_op jit(solution)/shard_map/pallas_call | solution.py:91
  50.8 3.4 %collective-permute-done.11 = bf16[128,512]{1,0:T(8,128)(2,1)S(1)} collective-permute-done((bf16[128,512]{1,0:T(8,128)(2,1)S(1)}, bf16[128,512]{1,0:T(8,128)(2,1)S(1)}, u32[]{:S(2)}, u32[]{:S(2)}) %collective-permute-start.11) | collective-permute-done | bytes 131104 | tf_op jit(solution)/shard_map/ppermute | solution.py:147
  54.2 0.8 %fusion.2 = f32[128,512]{1,0:T(8,128)} fusion(bf16[128,512]{1,0:T(8,128)(2,1)S(1)} %collective-permute-done.12, bf16[128,512]{1,0:T(8,128)(2,1)S(1)} %collective-permute-done.11, bf16[128,512]{1,0:T(8,128)(2,1)S(1)} %collective-permute-done.10, f32[4,128,512]{2,1,0:T(8,128)S(1)} %convert_add_fusion, s32[]{:T(128)S(6)} %select_n.42), kind=kLoop, calls=%fused_computation.4 | loop fusion | flops 458752 | bytes 917508 | tf_op jit(solution)/shard_map/div | solution.py:181
  (34 shorter events, 0.6 us)
Async XLA Ops:
  0.6 9.0 %copy-start = (bf16[128,4096]{1,0:T(8,128)(2,1)S(1)}, bf16[128,4096]{1,0:T(8,128)(2,1)}, u32[]{:S(2)}) copy-start(bf16[128,4096]{1,0:T(8,128)(2,1)} %param.5) | copy-start | bytes 3145732
  5.7 8.2 %copy-start.5 = (bf16[128,512]{1,0:T(8,128)(2,1)S(1)}, bf16[128,512]{1,0:T(8,128)(2,1)}, u32[]{:S(2)}) copy-start(bf16[128,512]{1,0:T(8,128)(2,1)} %get-tuple-element.15.refs_4_) | copy-start | bytes 393220
  5.7 8.7 %collective-permute-start.8 = (bf16[128,512]{1,0:T(8,128)(2,1)}, bf16[128,512]{1,0:T(8,128)(2,1)S(1)}, u32[]{:S(2)}, u32[]{:S(2)}) collective-permute-start(bf16[128,512]{1,0:T(8,128)(2,1)} %get-tuple-element.15.refs_4_), channel_id=1, source_target_pairs={{0,3},{1,2},{2,1},{3,0},{4,7},{5,6},{6,5},{7,4},{8,11},{9,10},{10,... | collective-permute-start | bytes 393224 | tf_op jit(solution)/shard_map/ppermute | solution.py:147
  10.4 17.3 %collective-permute-start.2 = (bf16[128,1024]{1,0:T(8,128)(2,1)S(1)}, bf16[128,1024]{1,0:T(8,128)(2,1)S(1)}, u32[]{:S(2)}, u32[]{:S(2)}) collective-permute-start(bf16[128,1024]{1,0:T(8,128)(2,1)S(1)} %get-tuple-element.21), channel_id=1, source_target_pairs={{0,3},{1,2},{2,1},{3,0},{4,7},{5,6},{6,5},{7,4},{8,11},{9,10},{10,... | collective-permute-start | bytes 786440 | tf_op jit(solution)/shard_map/ppermute | solution.py:147
  10.5 17.2 %collective-permute-start = (bf16[128,1024]{1,0:T(8,128)(2,1)S(1)}, bf16[128,1024]{1,0:T(8,128)(2,1)S(1)}, u32[]{:S(2)}, u32[]{:S(2)}) collective-permute-start(bf16[128,1024]{1,0:T(8,128)(2,1)S(1)} %get-tuple-element.22), channel_id=1, source_target_pairs={{0,1},{1,0},{2,3},{3,2},{4,5},{5,4},{6,7},{7,6},{8,9},{9,8},{10,11... | collective-permute-start | bytes 786440 | tf_op jit(solution)/shard_map/ppermute | solution.py:147
  12.4 15.3 %collective-permute-start.1 = (bf16[128,1024]{1,0:T(8,128)(2,1)S(1)}, bf16[128,1024]{1,0:T(8,128)(2,1)S(1)}, u32[]{:S(2)}, u32[]{:S(2)}) collective-permute-start(bf16[128,1024]{1,0:T(8,128)(2,1)S(1)} %get-tuple-element.24), channel_id=1, source_target_pairs={{0,2},{1,3},{2,0},{3,1},{4,6},{5,7},{6,4},{7,5},{8,10},{9,11},{10,... | collective-permute-start | bytes 786440 | tf_op jit(solution)/shard_map/ppermute | solution.py:147
  13.9 13.6 %collective-permute-start.7 = (bf16[128,512]{1,0:T(8,128)(2,1)S(1)}, bf16[128,512]{1,0:T(8,128)(2,1)S(1)}, u32[]{:S(2)}, u32[]{:S(2)}) collective-permute-start(bf16[128,512]{1,0:T(8,128)(2,1)S(1)} %copy-done.5), channel_id=1, source_target_pairs={{0,2},{1,3},{2,0},{3,1},{4,6},{5,7},{6,4},{7,5},{8,10},{9,11},{10,... | collective-permute-start | bytes 393224 | tf_op jit(solution)/shard_map/ppermute | solution.py:147
  14.4 13.3 %copy-start.6 = (bf16[128,512]{1,0:T(8,128)(2,1)}, bf16[128,512]{1,0:T(8,128)(2,1)S(1)}, u32[]{:S(2)}) copy-start(bf16[128,512]{1,0:T(8,128)(2,1)S(1)} %collective-permute-done.8.refs_7_) | copy-start | bytes 393220
  14.4 13.2 %collective-permute-start.6 = (bf16[128,512]{1,0:T(8,128)(2,1)S(1)}, bf16[128,512]{1,0:T(8,128)(2,1)S(1)}, u32[]{:S(2)}, u32[]{:S(2)}) collective-permute-start(bf16[128,512]{1,0:T(8,128)(2,1)S(1)} %copy-done.5), channel_id=1, source_target_pairs={{0,1},{1,0},{2,3},{3,2},{4,5},{5,4},{6,7},{7,6},{8,9},{9,8},{10,11... | collective-permute-start | bytes 393224 | tf_op jit(solution)/shard_map/ppermute | solution.py:147
  27.5 0.6 %copy-start.7 = (bf16[128,512]{1,0:T(8,128)(2,1)}, bf16[128,512]{1,0:T(8,128)(2,1)S(1)}, u32[]{:S(2)}) copy-start(bf16[128,512]{1,0:T(8,128)(2,1)S(1)} %collective-permute-done.7.refs_6_) | copy-start | bytes 393220
  27.7 0.7 %copy-start.9 = (bf16[128,512]{1,0:T(8,128)(2,1)}, bf16[128,512]{1,0:T(8,128)(2,1)S(1)}, u32[]{:S(2)}) copy-start(bf16[128,512]{1,0:T(8,128)(2,1)S(1)} %collective-permute-done.6.refs_5_) | copy-start | bytes 393220
  27.7 0.7 %copy-start.2 = (bf16[128,1024]{1,0:T(8,128)(2,1)}, bf16[128,1024]{1,0:T(8,128)(2,1)S(1)}, u32[]{:S(2)}) copy-start(bf16[128,1024]{1,0:T(8,128)(2,1)S(1)} %collective-permute-done.2.refs_3_) | copy-start | bytes 786436
  27.7 0.8 %copy-start.3 = (bf16[128,1024]{1,0:T(8,128)(2,1)}, bf16[128,1024]{1,0:T(8,128)(2,1)S(1)}, u32[]{:S(2)}) copy-start(bf16[128,1024]{1,0:T(8,128)(2,1)S(1)} %collective-permute-done.refs_1_) | copy-start | bytes 786436
  27.7 0.9 %copy-start.4 = (bf16[128,1024]{1,0:T(8,128)(2,1)}, bf16[128,1024]{1,0:T(8,128)(2,1)S(1)}, u32[]{:S(2)}) copy-start(bf16[128,1024]{1,0:T(8,128)(2,1)S(1)} %collective-permute-done.1.refs_2_) | copy-start | bytes 786436
  31.8 6.5 %collective-permute-start.9 = (bf16[4,128,512]{2,1,0:T(8,128)(2,1)}, bf16[4,128,512]{2,1,0:T(8,128)(2,1)S(1)}, u32[]{:S(2)}, u32[]{:S(2)}) collective-permute-start(bf16[4,128,512]{2,1,0:T(8,128)(2,1)} %get-tuple-element.17), channel_id=1, source_target_pairs={{0,4},{4,0},{8,12},{12,8},{16,20},{20,16},{24,28},{28,24},{1,5},{5... | collective-permute-start | bytes 1572872 | tf_op jit(solution)/shard_map/ppermute | solution.py:147
  31.8 6.5 %copy-start.1 = (f32[4,128,512]{2,1,0:T(8,128)S(1)}, f32[4,128,512]{2,1,0:T(8,128)}, u32[]{:S(2)}) copy-start(f32[4,128,512]{2,1,0:T(8,128)} %get-tuple-element.16) | copy-start | bytes 3145732
  34.8 7.9 %collective-permute-start.3 = (bf16[128,512]{1,0:T(8,128)(2,1)}, bf16[128,512]{1,0:T(8,128)(2,1)S(1)}, u32[]{:S(2)}, u32[]{:S(2)}) collective-permute-start(bf16[128,512]{1,0:T(8,128)(2,1)} %get-tuple-element.12), channel_id=1, source_target_pairs={{0,1},{1,0},{2,3},{3,2},{4,5},{5,4},{6,7},{7,6},{8,9},{9,8},{10,11... | collective-permute-start | bytes 393224 | tf_op jit(solution)/shard_map/ppermute | solution.py:147
  36.3 8.6 %collective-permute-start.4 = (bf16[128,512]{1,0:T(8,128)(2,1)}, bf16[128,512]{1,0:T(8,128)(2,1)S(1)}, u32[]{:S(2)}, u32[]{:S(2)}) collective-permute-start(bf16[128,512]{1,0:T(8,128)(2,1)} %get-tuple-element.13), channel_id=1, source_target_pairs={{0,2},{1,3},{2,0},{3,1},{4,6},{5,7},{6,4},{7,5},{8,10},{9,11},{10,... | collective-permute-start | bytes 393224 | tf_op jit(solution)/shard_map/ppermute | solution.py:147
  37.8 7.2 %collective-permute-start.5 = (bf16[128,512]{1,0:T(8,128)(2,1)}, bf16[128,512]{1,0:T(8,128)(2,1)S(1)}, u32[]{:S(2)}, u32[]{:S(2)}) collective-permute-start(bf16[128,512]{1,0:T(8,128)(2,1)} %get-tuple-element.14), channel_id=1, source_target_pairs={{0,3},{1,2},{2,1},{3,0},{4,7},{5,6},{6,5},{7,4},{8,11},{9,10},{10,... | collective-permute-start | bytes 393224 | tf_op jit(solution)/shard_map/ppermute | solution.py:147
  38.5 12.2 %collective-permute-start.10 = (bf16[128,512]{1,0:T(8,128)(2,1)S(1)}, bf16[128,512]{1,0:T(8,128)(2,1)S(1)}, u32[]{:S(2)}, u32[]{:S(2)}) collective-permute-start(bf16[128,512]{1,0:T(8,128)(2,1)S(1)} %get-tuple-element.18), channel_id=1, source_target_pairs={{0,8},{4,12},{8,0},{12,4},{16,24},{20,28},{24,16},{28,20},{1,9},{5... | collective-permute-start | bytes 393224 | tf_op jit(solution)/shard_map/ppermute | solution.py:147
  40.2 10.6 %collective-permute-start.12 = (bf16[128,512]{1,0:T(8,128)(2,1)S(1)}, bf16[128,512]{1,0:T(8,128)(2,1)S(1)}, u32[]{:S(2)}, u32[]{:S(2)}) collective-permute-start(bf16[128,512]{1,0:T(8,128)(2,1)S(1)} %get-tuple-element.19), channel_id=1, source_target_pairs={{0,24},{4,28},{8,16},{12,20},{16,8},{20,12},{24,0},{28,4},{1,25},{... | collective-permute-start | bytes 393224 | tf_op jit(solution)/shard_map/ppermute | solution.py:147
  42.7 2.3 %copy-start.8 = (bf16[128,512]{1,0:T(8,128)(2,1)}, bf16[128,512]{1,0:T(8,128)(2,1)S(1)}, u32[]{:S(2)}) copy-start(bf16[128,512]{1,0:T(8,128)(2,1)S(1)} %collective-permute-done.3.rest_1_) | copy-start | bytes 393220
  42.7 11.6 %collective-permute-start.11 = (bf16[128,512]{1,0:T(8,128)(2,1)S(1)}, bf16[128,512]{1,0:T(8,128)(2,1)S(1)}, u32[]{:S(2)}, u32[]{:S(2)}) collective-permute-start(bf16[128,512]{1,0:T(8,128)(2,1)S(1)} %get-tuple-element.20), channel_id=1, source_target_pairs={{0,16},{4,20},{8,24},{12,28},{16,0},{20,4},{24,8},{28,12},{1,17},{... | collective-permute-start | bytes 393224 | tf_op jit(solution)/shard_map/ppermute | solution.py:147
  44.9 0.7 %copy-start.11 = (bf16[128,512]{1,0:T(8,128)(2,1)}, bf16[128,512]{1,0:T(8,128)(2,1)S(1)}, u32[]{:S(2)}) copy-start(bf16[128,512]{1,0:T(8,128)(2,1)S(1)} %collective-permute-done.5.rest_3_) | copy-start | bytes 393220
  (1 other events, 0.6 us)

commit v2 on v1

v2 whole, which is shorter than its diff:
```python
import functools

import jax
import jax.numpy as jnp
from jax import lax
from jax.experimental import pallas as pl
from jax.experimental.pallas import tpu as pltpu
from jax.sharding import PartitionSpec as P

QUERY_HEADS = 32
KEY_VALUE_HEADS = 4
HEAD_SIZE = 128
GROUP = QUERY_HEADS // KEY_VALUE_HEADS
FACTOR = HEAD_SIZE ** (-0.5)
LOG2_E = 1.4426950408889634
VMEM = pl.BlockSpec(memory_space=pltpu.VMEM)


def dot(a, b):
    return jnp.dot(a, b, preferred_element_type=jnp.float32)


def dot_nt(a, b):
    return lax.dot_general(a, b, (((1,), (1,)), ((), ())), preferred_element_type=jnp.float32)


def dot_tn(a, b):
    return lax.dot_general(a, b, (((0,), (0,)), ((), ())), preferred_element_type=jnp.float32)


def head(ref, h):
    return ref[:, h * HEAD_SIZE : (h + 1) * HEAD_SIZE]


def stack(ref, first, count):
    return jnp.concatenate([head(ref, first + i) for i in range(count)], axis=0)


def call(kernel, out_shape, flops, arguments, in_specs=None, scratch=()):
    return pl.pallas_call(
        kernel,
        in_specs=in_specs or [VMEM] * len(arguments),
        out_specs=[VMEM] * len(out_shape),
        out_shape=out_shape,
        scratch_shapes=scratch,
        compiler_params=pltpu.CompilerParams(vmem_limit_bytes=40 << 20),
        cost_estimate=pl.CostEstimate(flops=flops, bytes_accessed=1_000_000, transcendentals=0),
    )(*arguments)


def struct(shape, dtype):
    return jax.ShapeDtypeStruct(shape, dtype)


def pack_kernel(nodes, source_ref, *refs):
    outs, sems = refs[:nodes], refs[nodes]
    node = lax.axis_index("node")
    width = outs[0].shape[1]
    copies = []
    for k in (*range(1, nodes), 0):
        columns = pl.ds(pl.multiple_of((node ^ k) * width, width), width)
        copies.append(pltpu.make_async_copy(source_ref.at[:, columns], outs[k], sems.at[k]))
        copies[-1].start()
    for copy in copies:
        copy.wait()


def pack_call(inputs, nodes):
    shape = (inputs.shape[0], inputs.shape[1] // nodes)
    return call(
        functools.partial(pack_kernel, nodes),
        [struct(shape, inputs.dtype)] * nodes,
        500_000_000,
        (inputs,),
        [pl.BlockSpec(memory_space=pl.ANY)],
        [pltpu.SemaphoreType.DMA((nodes,))],
    )


def softmax_kernel(q_ref, k_ref, g_ref, dv_ref, p_ref):
    tokens = q_ref.shape[0]
    wide = (tokens, GROUP * tokens)
    query = lax.broadcasted_iota(jnp.int32, wide, 1) % tokens
    seen = lax.broadcasted_iota(jnp.int32, wide, 0) <= query
    for g in range(KEY_VALUE_HEADS):
        scores = jnp.where(seen, dot_nt(head(k_ref, g), stack(q_ref, g * GROUP, GROUP)), -1e30)
        exponent = jnp.exp2((scores - jnp.max(scores, axis=0, keepdims=True)) * (FACTOR * LOG2_E))
        attention = exponent * (1.0 / jnp.sum(exponent, axis=0, keepdims=True))
        p_ref[:, g * wide[1] : (g + 1) * wide[1]] = attention
        d_values = dot(attention.astype(jnp.bfloat16), stack(g_ref, g * GROUP, GROUP))
        dv_ref[:, g * HEAD_SIZE : (g + 1) * HEAD_SIZE] = d_values.astype(jnp.bfloat16)


def softmax_call(queries, keys, gradient):
    tokens = queries.shape[0]
    outs = [struct(keys.shape, jnp.bfloat16), struct((tokens, QUERY_HEADS * tokens), jnp.float32)]
    return call(softmax_kernel, outs, 3_000_000_000, (queries, keys, gradient))


def key_kernel(q_ref, g_ref, p_ref, *rest):
    value_refs, out_ref = rest[:-1], rest[-1]
    wide = GROUP * q_ref.shape[0]
    for g in range(KEY_VALUE_HEADS):
        value = sum(head(ref, g).astype(jnp.float32) for ref in value_refs).astype(jnp.bfloat16)
        attention = p_ref[:, g * wide : (g + 1) * wide]
        d_attention = dot_nt(value, stack(g_ref, g * GROUP, GROUP))
        row_dots = jnp.sum(attention * d_attention, axis=0, keepdims=True)
        d_scores = (attention * (d_attention - row_dots)).astype(jnp.bfloat16)
        gradient = dot(d_scores, stack(q_ref, g * GROUP, GROUP)) * FACTOR
        out_ref[:, g * HEAD_SIZE : (g + 1) * HEAD_SIZE] = gradient.astype(jnp.bfloat16)


def key_call(queries, gradient, attention, values):
    outs = [struct(values[0].shape, jnp.bfloat16)]
    return call(key_kernel, outs, 2_500_000_000, (queries, gradient, attention, *values))[0]


def values_kernel(*refs):
    n = len(refs) // 2
    weights = refs[n][...]
    for source, out in zip(refs[:n], refs[n + 1 :]):
        out[...] = dot(source[...], weights).astype(out.dtype)


def values_call(blocks, weights):
    n = len(blocks)
    shape = (blocks[0].shape[0], weights.shape[1])
    outs = [struct(shape, jnp.float32 if i == 0 else jnp.bfloat16) for i in range(n)]
    return call(values_kernel, outs, 1_500_000_000, (*blocks, weights))


def weight_kernel(n, other, owners, *refs):
    blocks, d_values, out_ref = refs[:n], refs[n : 2 * n], refs[-1]
    chips, rows, width = out_ref.shape
    core = (lax.axis_index("dp") + other) % 2
    columns = [pl.ds(pl.multiple_of((2 * i + core) * rows, rows), rows) for i in range(chips)]
    source = jnp.concatenate(
        [jnp.concatenate([ref[:, c] for c in columns], axis=1) for ref in blocks], axis=0
    )
    product = dot_tn(source, jnp.concatenate([ref[...] for ref in d_values], axis=0))
    out_ref[...] = product.reshape(chips, rows, width).astype(out_ref.dtype)


def weight_call(blocks, d_values, other, owners, dtype, after=()):
    shape = (owners // 2, blocks[0].shape[1] // owners, d_values[0].shape[1])
    kernel = functools.partial(weight_kernel, len(blocks), other, owners)
    in_specs = [VMEM] * (2 * len(blocks)) + [pl.BlockSpec(memory_space=pl.ANY)] * len(after)
    return call(kernel, [struct(shape, dtype)], 1_000_000_000, (*blocks, *d_values, *after), in_specs)[0]


def swap(array, axis, distance):
    size = lax.axis_size(axis)
    return lax.ppermute(array, axis, [(i, i ^ distance) for i in range(size)])


def per_device(inputs, queries, keys, attention_gradient, value_matrix):
    nodes, owners = lax.axis_size("node"), lax.axis_size("dp")
    owner = lax.axis_index("dp")
    width = inputs.shape[1] // nodes

    packed = pack_call(inputs, nodes)
    blocks = [packed[0]] + [swap(packed[k], "node", k) for k in range(1, nodes)]
    d_values, attention = softmax_call(queries, keys, attention_gradient)
    all_d_values = [d_values] + [swap(d_values, "node", k) for k in range(1, nodes)]
    parts = values_call(blocks, value_matrix)
    values = [parts[0]] + [swap(parts[k], "node", k) for k in range(1, nodes)]
    key_gradient = key_call(queries, attention_gradient, attention, values)

    rows = width // owners
    if rows % 16 or owners % 2:
        local = dot_tn(jnp.concatenate(blocks, axis=0), jnp.concatenate(all_d_values, axis=0))
        owned = lax.psum_scatter(local, "dp", scatter_dimension=0, tiled=True)
        return key_gradient, owned / (owners * nodes)
    chip, chips = owner // 2, owners // 2
    send = weight_call(blocks, all_d_values, 1, owners, jnp.bfloat16, (parts[0],))
    keep = weight_call(blocks, all_d_values, 0, owners, jnp.float32)
    pair = keep + swap(send, "dp", 1).astype(jnp.float32)

    def chip_rows(other):
        return lax.dynamic_index_in_dim(pair, other, axis=0, keepdims=False)

    owned = chip_rows(chip)
    for k in range(1, chips):
        owned += swap(chip_rows(chip ^ k).astype(jnp.bfloat16), "dp", 2 * k).astype(jnp.float32)
    return key_gradient, owned / (owners * nodes)


def solution(mesh):
    placed = (
        P(("dp", "node"), None),
        P(("dp", "node"), None),
        P(("dp", "node"), None),
        P(("dp", "node"), None),
        P("node", None),
    )
    return jax.shard_map(
        per_device,
        mesh=mesh,
        in_specs=placed,
        out_specs=(P(("dp", "node"), None), P(("node", "dp"), None)),
        check_vma=False,
    )
```

time: 55.3 us -> 45.6 us (0.82)
  Pallas kernels: 16.4 us -> 5.3 us
  local copies, waits for them, and re-layouts: 2.42 us -> 4.74 us
  starting transfers between devices: 18.5 us -> 16.4 us
  waiting for transfers between devices: 16 us -> 17.2 us
    pallas_call x4 -> x6, Pallas kernels: 16.4 us -> 5.3 us  [call(): pl.pallas_call(kernel, in_specs=in_specs or [VMEM] * len(arguments), out_...]
    unnamed x24 -> x18, local copies, waits for them, and re-layouts: 1.57 us -> 4.68 us
    ppermute x13, starting transfers between devices: 18.5 us -> 16.4 us  [swap(): return lax.ppermute(array, axis, [(i, i ^ distance) for i in range(size)])]
    ppermute x13, waiting for transfers between devices: 16 us -> 17.2 us  [swap(): return lax.ppermute(array, axis, [(i, i ^ distance) for i in range(size)])]
    dynamic_slice x1 -> x0, local copies, waits for them, and re-layouts: 0.8 us -> none  [columns_of(): return lax.dynamic_slice_in_dim(inputs, other * width, width, axis=1)]
  transfers between devices with their start and end apart: 13 -> 13, of which waited for: 4 -> 5; matrix products, arithmetic and copies ran while one was open for 2% -> 1% of each run, Pallas kernels for 15% -> 10%
where the time goes in v2:
time: 45.6 us; the launch traced here: 45.3 us
  waiting for transfers between devices  17.2 us (38%)
  starting transfers between devices  16.4 us (36%)
  Pallas kernels  5.3 us (12%)
  local copies, waits for them, and re-layouts  4.74 us (10%)
  other arithmetic  0.94 us (2%)
  between operations  0.79 us (2%)
    ppermute x13, waiting for transfers between devices, swap(): return lax.ppermute(array, axis, [(i, i ^ distance) for i in range(size)])  17.2 us
    ppermute x13, starting transfers between devices, swap(): return lax.ppermute(array, axis, [(i, i ^ distance) for i in range(size)])  16.4 us
    pallas_call x6, Pallas kernels, call(): pl.pallas_call(kernel, in_specs=in_specs or [VMEM] * len(arguments), out_...  5.3 us
    unnamed x18, local copies, waits for them, and re-layouts  4.68 us
  transfers between devices with their start and end apart: 13, of which 5 were waited for; matrix products, arithmetic and copies ran while one was open for 1% of the time, Pallas kernels for 10%

profile of v2, /device:TPU:0, one launch (start us, length us, event | category | flops | bytes accessed | tf_op | source)
XLA Modules:
  0.0 45.3 jit_solution(12032281247589119526)
XLA Ops:
  0.6 1.2 %copy-done = bf16[128,4096]{1,0:T(8,128)(2,1)S(1)} copy-done((bf16[128,4096]{1,0:T(8,128)(2,1)S(1)}, bf16[128,4096]{1,0:T(8,128)(2,1)}, u32[]{:S(2)}) %copy-start) | copy-done | bytes 1048600
  2.0 3.0 %collective-permute-start = (bf16[128,1024]{1,0:T(8,128)(2,1)S(1)}, bf16[128,1024]{1,0:T(8,128)(2,1)S(1)}, u32[]{:S(2)}, u32[]{:S(2)}) collective-permute-start(bf16[128,1024]{1,0:T(8,128)(2,1)S(1)} %get-tuple-element.14), channel_id=1, source_target_pairs={{0,1},{1,0},{2,3},{3,2},{4,5},{5,4},{6,7},{7,6},{8,9},{9,8},{10,11... | collective-permute-start | bytes 786440 | tf_op jit(solution)/shard_map/ppermute | solution.py:153
  5.0 1.5 %collective-permute-start.1 = (bf16[128,1024]{1,0:T(8,128)(2,1)S(1)}, bf16[128,1024]{1,0:T(8,128)(2,1)S(1)}, u32[]{:S(2)}, u32[]{:S(2)}) collective-permute-start(bf16[128,1024]{1,0:T(8,128)(2,1)S(1)} %get-tuple-element.15), channel_id=1, source_target_pairs={{0,2},{1,3},{2,0},{3,1},{4,6},{5,7},{6,4},{7,5},{8,10},{9,11},{10,... | collective-permute-start | bytes 786440 | tf_op jit(solution)/shard_map/ppermute | solution.py:153
  6.5 1.3 %copy-done.2 = bf16[128,4096]{1,0:T(8,128)(2,1)S(1)} copy-done((bf16[128,4096]{1,0:T(8,128)(2,1)S(1)}, bf16[128,4096]{1,0:T(8,128)(2,1)}, u32[]{:S(2)}) %copy-start.2) | copy-done | bytes 1048600
  7.8 1.2 %copy-done.4 = bf16[128,4096]{1,0:T(8,128)(2,1)S(1)} copy-done((bf16[128,4096]{1,0:T(8,128)(2,1)S(1)}, bf16[128,4096]{1,0:T(8,128)(2,1)}, u32[]{:S(2)}) %copy-start.4) | copy-done | bytes 1048600
  9.1 0.9 %copy-done.6 = bf16[128,512]{1,0:T(8,128)(2,1)S(1)} copy-done((bf16[128,512]{1,0:T(8,128)(2,1)S(1)}, bf16[128,512]{1,0:T(8,128)(2,1)}, u32[]{:S(2)}) %copy-start.6) | copy-done | bytes 131096
  10.0 1.6 %shard_map.68 = (bf16[128,512]{1,0:T(8,128)(2,1)S(1)}, f32[128,4096]{1,0:T(8,128)S(1)}) custom-call(bf16[128,4096]{1,0:T(8,128)(2,1)S(1)} %copy-done.2, bf16[128,512]{1,0:T(8,128)(2,1)S(1)} %copy-done.6, bf16[128,4096]{1,0:T(8,128)(2,1)S(1)} %copy-done.4), custom_call_target="tpu_custom_call" | custom-call | flops 3000000000 | bytes 1000000 | tf_op jit(solution)/shard_map/pallas_call | solution.py:40
  11.6 2.9 %collective-permute-start.8 = (bf16[128,512]{1,0:T(8,128)(2,1)S(1)}, bf16[128,512]{1,0:T(8,128)(2,1)S(1)}, u32[]{:S(2)}, u32[]{:S(2)}) collective-permute-start(bf16[128,512]{1,0:T(8,128)(2,1)S(1)} %get-tuple-element.21.refs_4_), channel_id=1, source_target_pairs={{0,3},{1,2},{2,1},{3,0},{4,7},{5,6},{6,5},{7,4},{8,11},{9,10},{10,... | collective-permute-start | bytes 393224 | tf_op jit(solution)/shard_map/ppermute | solution.py:153
  14.5 0.5 %collective-permute-start.7 = (bf16[128,512]{1,0:T(8,128)(2,1)S(1)}, bf16[128,512]{1,0:T(8,128)(2,1)S(1)}, u32[]{:S(2)}, u32[]{:S(2)}) collective-permute-start(bf16[128,512]{1,0:T(8,128)(2,1)S(1)} %get-tuple-element.21.refs_4_), channel_id=1, source_target_pairs={{0,2},{1,3},{2,0},{3,1},{4,6},{5,7},{6,4},{7,5},{8,10},{9,11},{10,... | collective-permute-start | bytes 393224 | tf_op jit(solution)/shard_map/ppermute | solution.py:153
  15.1 6.4 %collective-permute-done.1.refs_2_ = bf16[128,1024]{1,0:T(8,128)(2,1)S(1)} collective-permute-done((bf16[128,1024]{1,0:T(8,128)(2,1)S(1)}, bf16[128,1024]{1,0:T(8,128)(2,1)S(1)}, u32[]{:S(2)}, u32[]{:S(2)}) %collective-permute-start.1) | collective-permute-done | bytes 262176 | tf_op jit(solution)/shard_map/ppermute | solution.py:153
  21.6 0.7 %shard_map.70 = (f32[128,512]{1,0:T(8,128)S(1)}, bf16[128,512]{1,0:T(8,128)(2,1)S(1)}, bf16[128,512]{1,0:T(8,128)(2,1)S(1)}, bf16[128,512]{1,0:T(8,128)(2,1)S(1)}) custom-call(bf16[128,1024]{1,0:T(8,128)(2,1)S(1)} %get-tuple-element.13.refs_0_, bf16[128,1024]{1,0:T(8,128)(2,1)S(1)} %collective-permute-done.refs_1_, ...), custom_call_target="tpu_custom_call" | custom-call | flops 1500000000 | bytes 1000000 | tf_op jit(solution)/shard_map/pallas_call | solution.py:40
  22.3 1.7 %collective-permute-done.7.refs_6_ = bf16[128,512]{1,0:T(8,128)(2,1)S(1)} collective-permute-done((bf16[128,512]{1,0:T(8,128)(2,1)S(1)}, bf16[128,512]{1,0:T(8,128)(2,1)S(1)}, u32[]{:S(2)}, u32[]{:S(2)}) %collective-permute-start.7) | collective-permute-done | bytes 131104 | tf_op jit(solution)/shard_map/ppermute | solution.py:153
  24.0 0.5 %shard_map.73 = bf16[4,128,512]{2,1,0:T(8,128)(2,1)S(1)} custom-call(bf16[128,1024]{1,0:T(8,128)(2,1)S(1)} %get-tuple-element.13.refs_0_, bf16[128,1024]{1,0:T(8,128)(2,1)S(1)} %collective-permute-done.refs_1_, bf16[128,1024]{1,0:T(8,128)(2,1)S(1)} %collective-permute-done.1.refs_2_, bf16[128,1024]{1,0:T(8,128)(2,1)S(1)} %collective-permute-done.2.refs_3_, ...), custom_call_target="tpu_custom_call" | custom-call | flops 1000000000 | bytes 1000000 | tf_op jit(solution)/shard_map/pallas_call | solution.py:40
  24.6 1.3 %collective-permute-start.3 = (bf16[128,512]{1,0:T(8,128)(2,1)S(1)}, bf16[128,512]{1,0:T(8,128)(2,1)S(1)}, u32[]{:S(2)}, u32[]{:S(2)}) collective-permute-start(bf16[128,512]{1,0:T(8,128)(2,1)S(1)} %get-tuple-element.18), channel_id=1, source_target_pairs={{0,1},{1,0},{2,3},{3,2},{4,5},{5,4},{6,7},{7,6},{8,9},{9,8},{10,11... | collective-permute-start | bytes 393224 | tf_op jit(solution)/shard_map/ppermute | solution.py:153
  25.9 0.8 %collective-permute-start.4 = (bf16[128,512]{1,0:T(8,128)(2,1)S(1)}, bf16[128,512]{1,0:T(8,128)(2,1)S(1)}, u32[]{:S(2)}, u32[]{:S(2)}) collective-permute-start(bf16[128,512]{1,0:T(8,128)(2,1)S(1)} %get-tuple-element.19), channel_id=1, source_target_pairs={{0,2},{1,3},{2,0},{3,1},{4,6},{5,7},{6,4},{7,5},{8,10},{9,11},{10,... | collective-permute-start | bytes 393224 | tf_op jit(solution)/shard_map/ppermute | solution.py:153
  26.7 1.4 %collective-permute-start.5 = (bf16[128,512]{1,0:T(8,128)(2,1)S(1)}, bf16[128,512]{1,0:T(8,128)(2,1)S(1)}, u32[]{:S(2)}, u32[]{:S(2)}) collective-permute-start(bf16[128,512]{1,0:T(8,128)(2,1)S(1)} %get-tuple-element.20), channel_id=1, source_target_pairs={{0,3},{1,2},{2,1},{3,0},{4,7},{5,6},{6,5},{7,4},{8,11},{9,10},{10,... | collective-permute-start | bytes 393224 | tf_op jit(solution)/shard_map/ppermute | solution.py:153
  28.9 1.6 %collective-permute-start.10 = (bf16[128,512]{1,0:T(8,128)(2,1)S(1)}, bf16[128,512]{1,0:T(8,128)(2,1)S(1)}, u32[]{:S(2)}, u32[]{:S(2)}) collective-permute-start(bf16[128,512]{1,0:T(8,128)(2,1)S(1)} %get-tuple-element.22), channel_id=1, source_target_pairs={{0,8},{4,12},{8,0},{12,4},{16,24},{20,28},{24,16},{28,20},{1,9},{5... | collective-permute-start | bytes 393224 | tf_op jit(solution)/shard_map/ppermute | solution.py:153
  30.6 2.5 %collective-permute-start.12 = (bf16[128,512]{1,0:T(8,128)(2,1)S(1)}, bf16[128,512]{1,0:T(8,128)(2,1)S(1)}, u32[]{:S(2)}, u32[]{:S(2)}) collective-permute-start(bf16[128,512]{1,0:T(8,128)(2,1)S(1)} %get-tuple-element.23), channel_id=1, source_target_pairs={{0,24},{4,28},{8,16},{12,20},{16,8},{20,12},{24,0},{28,4},{1,25},{... | collective-permute-start | bytes 393224 | tf_op jit(solution)/shard_map/ppermute | solution.py:153
  33.1 0.5 %collective-permute-start.11 = (bf16[128,512]{1,0:T(8,128)(2,1)S(1)}, bf16[128,512]{1,0:T(8,128)(2,1)S(1)}, u32[]{:S(2)}, u32[]{:S(2)}) collective-permute-start(bf16[128,512]{1,0:T(8,128)(2,1)S(1)} %get-tuple-element.24), channel_id=1, source_target_pairs={{0,16},{4,20},{8,24},{12,28},{16,0},{20,4},{24,8},{28,12},{1,17},{... | collective-permute-start | bytes 393224 | tf_op jit(solution)/shard_map/ppermute | solution.py:153
  33.6 0.7 %collective-permute-done.5.rest_3_ = bf16[128,512]{1,0:T(8,128)(2,1)S(1)} collective-permute-done((bf16[128,512]{1,0:T(8,128)(2,1)S(1)}, bf16[128,512]{1,0:T(8,128)(2,1)S(1)}, u32[]{:S(2)}, u32[]{:S(2)}) %collective-permute-start.5) | collective-permute-done | bytes 131104 | tf_op jit(solution)/shard_map/ppermute | solution.py:153
  34.3 1.9 %shard_map.71 = bf16[128,512]{1,0:T(8,128)(2,1)} custom-call(bf16[128,4096]{1,0:T(8,128)(2,1)S(1)} %copy-done.3, bf16[128,4096]{1,0:T(8,128)(2,1)S(1)} %copy-done.5, f32[128,4096]{1,0:T(8,128)S(1)} %copy-done.8, f32[128,512]{1,0:T(8,128)S(1)} %get-tuple-element.17.rest_0_.refs_8_, bf16[128,512]{1,0:T(8,128)(2,1)S(1)} %collective-permute-done.3.rest_1_, ...), custom_call_target="tpu_custom_call" | custom-call | flops 2500000000 | bytes 1000000 | tf_op jit(solution)/shard_map/pallas_call | solution.py:40
  36.2 4.1 %collective-permute-done.12 = bf16[128,512]{1,0:T(8,128)(2,1)S(1)} collective-permute-done((bf16[128,512]{1,0:T(8,128)(2,1)S(1)}, bf16[128,512]{1,0:T(8,128)(2,1)S(1)}, u32[]{:S(2)}, u32[]{:S(2)}) %collective-permute-start.12) | collective-permute-done | bytes 131104 | tf_op jit(solution)/shard_map/ppermute | solution.py:153
  40.2 4.3 %collective-permute-done.11 = bf16[128,512]{1,0:T(8,128)(2,1)S(1)} collective-permute-done((bf16[128,512]{1,0:T(8,128)(2,1)S(1)}, bf16[128,512]{1,0:T(8,128)(2,1)S(1)}, u32[]{:S(2)}, u32[]{:S(2)}) %collective-permute-start.11) | collective-permute-done | bytes 131104 | tf_op jit(solution)/shard_map/ppermute | solution.py:153
  44.6 0.8 %fusion.2 = f32[128,512]{1,0:T(8,128)} fusion(bf16[128,512]{1,0:T(8,128)(2,1)S(1)} %collective-permute-done.12, bf16[128,512]{1,0:T(8,128)(2,1)S(1)} %collective-permute-done.11, bf16[128,512]{1,0:T(8,128)(2,1)S(1)} %collective-permute-done.10, f32[4,128,512]{2,1,0:T(8,128)S(1)} %convert_add_fusion, s32[]{:T(128)S(6)} %select_n.19), kind=kLoop, calls=%fused_computation.4 | loop fusion | flops 458752 | bytes 917508 | tf_op jit(solution)/shard_map/div | solution.py:185
  (29 shorter events, 1.1 us)
Async XLA Ops:
  0.6 1.2 %copy-start = (bf16[128,4096]{1,0:T(8,128)(2,1)S(1)}, bf16[128,4096]{1,0:T(8,128)(2,1)}, u32[]{:S(2)}) copy-start(bf16[128,4096]{1,0:T(8,128)(2,1)} %source_ref.1) | copy-start | bytes 3145732
  2.0 13.0 %collective-permute-start = (bf16[128,1024]{1,0:T(8,128)(2,1)S(1)}, bf16[128,1024]{1,0:T(8,128)(2,1)S(1)}, u32[]{:S(2)}, u32[]{:S(2)}) collective-permute-start(bf16[128,1024]{1,0:T(8,128)(2,1)S(1)} %get-tuple-element.14), channel_id=1, source_target_pairs={{0,1},{1,0},{2,3},{3,2},{4,5},{5,4},{6,7},{7,6},{8,9},{9,8},{10,11... | collective-permute-start | bytes 786440 | tf_op jit(solution)/shard_map/ppermute | solution.py:153
  5.0 16.6 %collective-permute-start.1 = (bf16[128,1024]{1,0:T(8,128)(2,1)S(1)}, bf16[128,1024]{1,0:T(8,128)(2,1)S(1)}, u32[]{:S(2)}, u32[]{:S(2)}) collective-permute-start(bf16[128,1024]{1,0:T(8,128)(2,1)S(1)} %get-tuple-element.15), channel_id=1, source_target_pairs={{0,2},{1,3},{2,0},{3,1},{4,6},{5,7},{6,4},{7,5},{8,10},{9,11},{10,... | collective-permute-start | bytes 786440 | tf_op jit(solution)/shard_map/ppermute | solution.py:153
  6.5 15.1 %copy-start.1 = (bf16[1024,512]{1,0:T(8,128)(2,1)S(1)}, bf16[1024,512]{1,0:T(8,128)(2,1)}, u32[]{:S(2)}) copy-start(bf16[1024,512]{1,0:T(8,128)(2,1)} %refs_4_.1) | copy-start | bytes 3145732
  6.5 15.1 %collective-permute-start.2 = (bf16[128,1024]{1,0:T(8,128)(2,1)S(1)}, bf16[128,1024]{1,0:T(8,128)(2,1)S(1)}, u32[]{:S(2)}, u32[]{:S(2)}) collective-permute-start(bf16[128,1024]{1,0:T(8,128)(2,1)S(1)} %get-tuple-element.16), channel_id=1, source_target_pairs={{0,3},{1,2},{2,1},{3,0},{4,7},{5,6},{6,5},{7,4},{8,11},{9,10},{10,... | collective-permute-start | bytes 786440 | tf_op jit(solution)/shard_map/ppermute | solution.py:153
  6.5 1.3 %copy-start.2 = (bf16[128,4096]{1,0:T(8,128)(2,1)S(1)}, bf16[128,4096]{1,0:T(8,128)(2,1)}, u32[]{:S(2)}) copy-start(bf16[128,4096]{1,0:T(8,128)(2,1)} %q_ref.3) | copy-start | bytes 3145732
  7.8 1.2 %copy-start.4 = (bf16[128,4096]{1,0:T(8,128)(2,1)S(1)}, bf16[128,4096]{1,0:T(8,128)(2,1)}, u32[]{:S(2)}) copy-start(bf16[128,4096]{1,0:T(8,128)(2,1)} %g_ref.3) | copy-start | bytes 3145732
  9.1 0.9 %copy-start.6 = (bf16[128,512]{1,0:T(8,128)(2,1)S(1)}, bf16[128,512]{1,0:T(8,128)(2,1)}, u32[]{:S(2)}) copy-start(bf16[128,512]{1,0:T(8,128)(2,1)} %k_ref.1) | copy-start | bytes 393220
  11.6 10.7 %copy-start.7 = (f32[128,4096]{1,0:T(8,128)}, f32[128,4096]{1,0:T(8,128)S(1)}, u32[]{:S(2)}) copy-start(f32[128,4096]{1,0:T(8,128)S(1)} %get-tuple-element.12.p_ref) | copy-start | bytes 6291460
  11.6 10.7 %collective-permute-start.8 = (bf16[128,512]{1,0:T(8,128)(2,1)S(1)}, bf16[128,512]{1,0:T(8,128)(2,1)S(1)}, u32[]{:S(2)}, u32[]{:S(2)}) collective-permute-start(bf16[128,512]{1,0:T(8,128)(2,1)S(1)} %get-tuple-element.21.refs_4_), channel_id=1, source_target_pairs={{0,3},{1,2},{2,1},{3,0},{4,7},{5,6},{6,5},{7,4},{8,11},{9,10},{10,... | collective-permute-start | bytes 393224 | tf_op jit(solution)/shard_map/ppermute | solution.py:153
  14.5 9.5 %collective-permute-start.7 = (bf16[128,512]{1,0:T(8,128)(2,1)S(1)}, bf16[128,512]{1,0:T(8,128)(2,1)S(1)}, u32[]{:S(2)}, u32[]{:S(2)}) collective-permute-start(bf16[128,512]{1,0:T(8,128)(2,1)S(1)} %get-tuple-element.21.refs_4_), channel_id=1, source_target_pairs={{0,2},{1,3},{2,0},{3,1},{4,6},{5,7},{6,4},{7,5},{8,10},{9,11},{10,... | collective-permute-start | bytes 393224 | tf_op jit(solution)/shard_map/ppermute | solution.py:153
  15.0 9.0 %collective-permute-start.6 = (bf16[128,512]{1,0:T(8,128)(2,1)S(1)}, bf16[128,512]{1,0:T(8,128)(2,1)S(1)}, u32[]{:S(2)}, u32[]{:S(2)}) collective-permute-start(bf16[128,512]{1,0:T(8,128)(2,1)S(1)} %get-tuple-element.21.refs_4_), channel_id=1, source_target_pairs={{0,1},{1,0},{2,3},{3,2},{4,5},{5,4},{6,7},{7,6},{8,9},{9,8},{10,11... | collective-permute-start | bytes 393224 | tf_op jit(solution)/shard_map/ppermute | solution.py:153
  24.5 4.2 %collective-permute-start.9 = (bf16[4,128,512]{2,1,0:T(8,128)(2,1)S(1)}, bf16[4,128,512]{2,1,0:T(8,128)(2,1)S(1)}, u32[]{:S(2)}, u32[]{:S(2)}) collective-permute-start(bf16[4,128,512]{2,1,0:T(8,128)(2,1)S(1)} %shard_map.73), channel_id=1, source_target_pairs={{0,4},{4,0},{8,12},{12,8},{16,20},{20,16},{24,28},{28,24},{1,5},{5... | collective-permute-start | bytes 1572872 | tf_op jit(solution)/shard_map/ppermute | solution.py:153
  24.6 8.5 %collective-permute-start.3 = (bf16[128,512]{1,0:T(8,128)(2,1)S(1)}, bf16[128,512]{1,0:T(8,128)(2,1)S(1)}, u32[]{:S(2)}, u32[]{:S(2)}) collective-permute-start(bf16[128,512]{1,0:T(8,128)(2,1)S(1)} %get-tuple-element.18), channel_id=1, source_target_pairs={{0,1},{1,0},{2,3},{3,2},{4,5},{5,4},{6,7},{7,6},{8,9},{9,8},{10,11... | collective-permute-start | bytes 393224 | tf_op jit(solution)/shard_map/ppermute | solution.py:153
  25.9 7.7 %collective-permute-start.4 = (bf16[128,512]{1,0:T(8,128)(2,1)S(1)}, bf16[128,512]{1,0:T(8,128)(2,1)S(1)}, u32[]{:S(2)}, u32[]{:S(2)}) collective-permute-start(bf16[128,512]{1,0:T(8,128)(2,1)S(1)} %get-tuple-element.19), channel_id=1, source_target_pairs={{0,2},{1,3},{2,0},{3,1},{4,6},{5,7},{6,4},{7,5},{8,10},{9,11},{10,... | collective-permute-start | bytes 393224 | tf_op jit(solution)/shard_map/ppermute | solution.py:153
  26.7 7.5 %collective-permute-start.5 = (bf16[128,512]{1,0:T(8,128)(2,1)S(1)}, bf16[128,512]{1,0:T(8,128)(2,1)S(1)}, u32[]{:S(2)}, u32[]{:S(2)}) collective-permute-start(bf16[128,512]{1,0:T(8,128)(2,1)S(1)} %get-tuple-element.20), channel_id=1, source_target_pairs={{0,3},{1,2},{2,1},{3,0},{4,7},{5,6},{6,5},{7,4},{8,11},{9,10},{10,... | collective-permute-start | bytes 393224 | tf_op jit(solution)/shard_map/ppermute | solution.py:153
  28.2 6.1 %copy-start.8 = (f32[128,4096]{1,0:T(8,128)S(1)}, f32[128,4096]{1,0:T(8,128)}, u32[]{:S(2)}) copy-start(f32[128,4096]{1,0:T(8,128)} %copy-done.7) | copy-start | bytes 6291460
  28.6 5.6 %copy-start.3 = (bf16[128,4096]{1,0:T(8,128)(2,1)S(1)}, bf16[128,4096]{1,0:T(8,128)(2,1)}, u32[]{:S(2)}) copy-start(bf16[128,4096]{1,0:T(8,128)(2,1)} %q_ref.3) | copy-start | bytes 3145732
  28.7 5.6 %copy-start.5 = (bf16[128,4096]{1,0:T(8,128)(2,1)S(1)}, bf16[128,4096]{1,0:T(8,128)(2,1)}, u32[]{:S(2)}) copy-start(bf16[128,4096]{1,0:T(8,128)(2,1)} %g_ref.3) | copy-start | bytes 3145732
  28.9 7.2 %collective-permute-start.10 = (bf16[128,512]{1,0:T(8,128)(2,1)S(1)}, bf16[128,512]{1,0:T(8,128)(2,1)S(1)}, u32[]{:S(2)}, u32[]{:S(2)}) collective-permute-start(bf16[128,512]{1,0:T(8,128)(2,1)S(1)} %get-tuple-element.22), channel_id=1, source_target_pairs={{0,8},{4,12},{8,0},{12,4},{16,24},{20,28},{24,16},{28,20},{1,9},{5... | collective-permute-start | bytes 393224 | tf_op jit(solution)/shard_map/ppermute | solution.py:153
  30.6 9.7 %collective-permute-start.12 = (bf16[128,512]{1,0:T(8,128)(2,1)S(1)}, bf16[128,512]{1,0:T(8,128)(2,1)S(1)}, u32[]{:S(2)}, u32[]{:S(2)}) collective-permute-start(bf16[128,512]{1,0:T(8,128)(2,1)S(1)} %get-tuple-element.23), channel_id=1, source_target_pairs={{0,24},{4,28},{8,16},{12,20},{16,8},{20,12},{24,0},{28,4},{1,25},{... | collective-permute-start | bytes 393224 | tf_op jit(solution)/shard_map/ppermute | solution.py:153
  33.1 11.5 %collective-permute-start.11 = (bf16[128,512]{1,0:T(8,128)(2,1)S(1)}, bf16[128,512]{1,0:T(8,128)(2,1)S(1)}, u32[]{:S(2)}, u32[]{:S(2)}) collective-permute-start(bf16[128,512]{1,0:T(8,128)(2,1)S(1)} %get-tuple-element.24), channel_id=1, source_target_pairs={{0,16},{4,20},{8,24},{12,28},{16,0},{20,4},{24,8},{28,12},{1,17},{... | collective-permute-start | bytes 393224 | tf_op jit(solution)/shard_map/ppermute | solution.py:153

commit v3 on v2

--- a/solution.py
+++ b/solution.py
@@ -94,7 +94,7 @@
 def softmax_call(queries, keys, gradient):
     tokens = queries.shape[0]
     outs = [struct(keys.shape, jnp.bfloat16), struct((tokens, QUERY_HEADS * tokens), jnp.float32)]
-    return call(softmax_kernel, outs, 3_000_000_000, (queries, keys, gradient))
+    return call(softmax_kernel, outs, 3000000000, (queries, keys, gradient))
 
 
 def key_kernel(q_ref, g_ref, p_ref, *rest):
@@ -126,7 +126,7 @@
     n = len(blocks)
     shape = (blocks[0].shape[0], weights.shape[1])
     outs = [struct(shape, jnp.float32 if i == 0 else jnp.bfloat16) for i in range(n)]
-    return call(values_kernel, outs, 1_500_000_000, (*blocks, weights))
+    return call(values_kernel, outs, 1500000000, (*blocks, weights))
 
 
 def weight_kernel(n, other, owners, *refs):
@@ -141,11 +141,11 @@
     out_ref[...] = product.reshape(chips, rows, width).astype(out_ref.dtype)
 
 
-def weight_call(blocks, d_values, other, owners, dtype, after=()):
+def weight_call(blocks, d_values, other, owners, dtype, after=(), flops=1_000_000_000):
     shape = (owners // 2, blocks[0].shape[1] // owners, d_values[0].shape[1])
     kernel = functools.partial(weight_kernel, len(blocks), other, owners)
     in_specs = [VMEM] * (2 * len(blocks)) + [pl.BlockSpec(memory_space=pl.ANY)] * len(after)
-    return call(kernel, [struct(shape, dtype)], 1_000_000_000, (*blocks, *d_values, *after), in_specs)[0]
+    return call(kernel, [struct(shape, dtype)], flops, (*blocks, *d_values, *after), in_specs)[0]
 
 
 def swap(array, axis, distance):
@@ -160,9 +160,11 @@
 
     packed = pack_call(inputs, nodes)
     blocks = [packed[0]] + [swap(packed[k], "node", k) for k in range(1, nodes)]
+    order = [0, *range(nodes - 1, 0, -1)]
     d_values, attention = softmax_call(queries, keys, attention_gradient)
     all_d_values = [d_values] + [swap(d_values, "node", k) for k in range(1, nodes)]
-    parts = values_call(blocks, value_matrix)
+    parts = values_call([blocks[k] for k in order], value_matrix)
+    parts = [parts[order.index(k)] for k in range(nodes)]
     values = [parts[0]] + [swap(parts[k], "node", k) for k in range(1, nodes)]
     key_gradient = key_call(queries, attention_gradient, attention, values)
 
@@ -172,15 +174,15 @@
         owned = lax.psum_scatter(local, "dp", scatter_dimension=0, tiled=True)
         return key_gradient, owned / (owners * nodes)
     chip, chips = owner // 2, owners // 2
-    send = weight_call(blocks, all_d_values, 1, owners, jnp.bfloat16, (parts[0],))
-    keep = weight_call(blocks, all_d_values, 0, owners, jnp.float32)
+    send = weight_call([blocks[k] for k in order], [all_d_values[k] for k in order], 1, owners, jnp.bfloat16, (parts[0],))
+    keep = weight_call([blocks[k] for k in order], [all_d_values[k] for k in order], 0, owners, jnp.float32, (), 6000000000)
     pair = keep + swap(send, "dp", 1).astype(jnp.float32)
 
     def chip_rows(other):
         return lax.dynamic_index_in_dim(pair, other, axis=0, keepdims=False)
 
     owned = chip_rows(chip)
-    for k in range(1, chips):
+    for k in sorted(range(1, chips), key=lambda k: (k == chips - 1, k % 2)):
         owned += swap(chip_rows(chip ^ k).astype(jnp.bfloat16), "dp", 2 * k).astype(jnp.float32)
     return key_gradient, owned / (owners * nodes)
 

time: 45.6 us -> 42.3 us (0.928)
  waiting for transfers between devices: 17.2 us -> 12.3 us
  local copies, waits for them, and re-layouts: 4.74 us -> 6.05 us
    ppermute x13, waiting for transfers between devices: 17.2 us -> 12.3 us  [swap(): return lax.ppermute(array, axis, [(i, i ^ distance) for i in range(size)])]
    unnamed x18, local copies, waits for them, and re-layouts: 4.68 us -> 5.99 us
  transfers between devices with their start and end apart: 13 -> 13, of which waited for: 5 -> 6; matrix products, arithmetic and copies ran while one was open for 1% -> 1% of each run, Pallas kernels for 10% -> 12%
where the time goes in v3:
time: 42.3 us; the launch traced here: 41.8 us
  starting transfers between devices  16.4 us (39%)
  waiting for transfers between devices  12.3 us (29%)
  local copies, waits for them, and re-layouts  6.05 us (14%)
  Pallas kernels  5.32 us (13%)
  other arithmetic  0.94 us (2%)
  between operations  0.76 us (2%)
    ppermute x13, starting transfers between devices, swap(): return lax.ppermute(array, axis, [(i, i ^ distance) for i in range(size)])  16.4 us
    ppermute x13, waiting for transfers between devices, swap(): return lax.ppermute(array, axis, [(i, i ^ distance) for i in range(size)])  12.3 us
    unnamed x18, local copies, waits for them, and re-layouts  5.99 us
    pallas_call x6, Pallas kernels, call(): pl.pallas_call(kernel, in_specs=in_specs or [VMEM] * len(arguments), out_...  5.32 us
  transfers between devices with their start and end apart: 13, of which 6 were waited for; matrix products, arithmetic and copies ran while one was open for 1% of the time, Pallas kernels for 12%

profile of v3, /device:TPU:0, one launch (start us, length us, event | category | flops | bytes accessed | tf_op | source)
XLA Modules:
  0.0 41.8 jit_solution(5388510211244168531)
XLA Ops:
  0.6 1.2 %copy-done = bf16[128,4096]{1,0:T(8,128)(2,1)S(1)} copy-done((bf16[128,4096]{1,0:T(8,128)(2,1)S(1)}, bf16[128,4096]{1,0:T(8,128)(2,1)}, u32[]{:S(2)}) %copy-start) | copy-done | bytes 1048600
  2.0 4.0 %collective-permute-start = (bf16[128,1024]{1,0:T(8,128)(2,1)S(1)}, bf16[128,1024]{1,0:T(8,128)(2,1)S(1)}, u32[]{:S(2)}, u32[]{:S(2)}) collective-permute-start(bf16[128,1024]{1,0:T(8,128)(2,1)S(1)} %get-tuple-element.14), channel_id=1, source_target_pairs={{0,3},{1,2},{2,1},{3,0},{4,7},{5,6},{6,5},{7,4},{8,11},{9,10},{10,... | collective-permute-start | bytes 786440 | tf_op jit(solution)/shard_map/ppermute | solution.py:153
  5.9 0.5 %collective-permute-start.1 = (bf16[128,1024]{1,0:T(8,128)(2,1)S(1)}, bf16[128,1024]{1,0:T(8,128)(2,1)S(1)}, u32[]{:S(2)}, u32[]{:S(2)}) collective-permute-start(bf16[128,1024]{1,0:T(8,128)(2,1)S(1)} %get-tuple-element.15), channel_id=1, source_target_pairs={{0,2},{1,3},{2,0},{3,1},{4,6},{5,7},{6,4},{7,5},{8,10},{9,11},{10,... | collective-permute-start | bytes 786440 | tf_op jit(solution)/shard_map/ppermute | solution.py:153
  6.6 1.3 %copy-done.2 = bf16[128,4096]{1,0:T(8,128)(2,1)S(1)} copy-done((bf16[128,4096]{1,0:T(8,128)(2,1)S(1)}, bf16[128,4096]{1,0:T(8,128)(2,1)}, u32[]{:S(2)}) %copy-start.2) | copy-done | bytes 1048600
  7.9 1.2 %copy-done.4 = bf16[128,4096]{1,0:T(8,128)(2,1)S(1)} copy-done((bf16[128,4096]{1,0:T(8,128)(2,1)S(1)}, bf16[128,4096]{1,0:T(8,128)(2,1)}, u32[]{:S(2)}) %copy-start.4) | copy-done | bytes 1048600
  9.1 0.9 %copy-done.6 = bf16[128,512]{1,0:T(8,128)(2,1)S(1)} copy-done((bf16[128,512]{1,0:T(8,128)(2,1)S(1)}, bf16[128,512]{1,0:T(8,128)(2,1)}, u32[]{:S(2)}) %copy-start.6) | copy-done | bytes 131096
  10.0 1.6 %shard_map.68 = (bf16[128,512]{1,0:T(8,128)(2,1)S(1)}, f32[128,4096]{1,0:T(8,128)S(1)}) custom-call(bf16[128,4096]{1,0:T(8,128)(2,1)S(1)} %copy-done.2, bf16[128,512]{1,0:T(8,128)(2,1)S(1)} %copy-done.6, bf16[128,4096]{1,0:T(8,128)(2,1)S(1)} %copy-done.4), custom_call_target="tpu_custom_call" | custom-call | flops 3000000000 | bytes 1000000 | tf_op jit(solution)/shard_map/pallas_call | solution.py:40
  11.6 1.3 %copy-done.7 = f32[128,4096]{1,0:T(8,128)} copy-done((f32[128,4096]{1,0:T(8,128)}, f32[128,4096]{1,0:T(8,128)S(1)}, u32[]{:S(2)}) %copy-start.7) | copy-done | bytes 2097176
  13.0 1.8 %collective-permute-start.8 = (bf16[128,512]{1,0:T(8,128)(2,1)S(1)}, bf16[128,512]{1,0:T(8,128)(2,1)S(1)}, u32[]{:S(2)}, u32[]{:S(2)}) collective-permute-start(bf16[128,512]{1,0:T(8,128)(2,1)S(1)} %get-tuple-element.21.refs_4_), channel_id=1, source_target_pairs={{0,1},{1,0},{2,3},{3,2},{4,5},{5,4},{6,7},{7,6},{8,9},{9,8},{10,11... | collective-permute-start | bytes 393224 | tf_op jit(solution)/shard_map/ppermute | solution.py:153
  14.8 1.5 %collective-permute-start.7 = (bf16[128,512]{1,0:T(8,128)(2,1)S(1)}, bf16[128,512]{1,0:T(8,128)(2,1)S(1)}, u32[]{:S(2)}, u32[]{:S(2)}) collective-permute-start(bf16[128,512]{1,0:T(8,128)(2,1)S(1)} %get-tuple-element.21.refs_4_), channel_id=1, source_target_pairs={{0,2},{1,3},{2,0},{3,1},{4,6},{5,7},{6,4},{7,5},{8,10},{9,11},{10,... | collective-permute-start | bytes 393224 | tf_op jit(solution)/shard_map/ppermute | solution.py:153
  16.5 1.5 %collective-permute-done.1.refs_2_ = bf16[128,1024]{1,0:T(8,128)(2,1)S(1)} collective-permute-done((bf16[128,1024]{1,0:T(8,128)(2,1)S(1)}, bf16[128,1024]{1,0:T(8,128)(2,1)S(1)}, u32[]{:S(2)}, u32[]{:S(2)}) %collective-permute-start.1) | collective-permute-done | bytes 262176 | tf_op jit(solution)/shard_map/ppermute | solution.py:153
  18.0 1.3 %collective-permute-done.2.refs_3_ = bf16[128,1024]{1,0:T(8,128)(2,1)S(1)} collective-permute-done((bf16[128,1024]{1,0:T(8,128)(2,1)S(1)}, bf16[128,1024]{1,0:T(8,128)(2,1)S(1)}, u32[]{:S(2)}, u32[]{:S(2)}) %collective-permute-start.2) | collective-permute-done | bytes 262176 | tf_op jit(solution)/shard_map/ppermute | solution.py:153
  19.3 0.7 %shard_map.70 = (f32[128,512]{1,0:T(8,128)S(1)}, bf16[128,512]{1,0:T(8,128)(2,1)S(1)}, bf16[128,512]{1,0:T(8,128)(2,1)S(1)}, bf16[128,512]{1,0:T(8,128)(2,1)S(1)}) custom-call(bf16[128,1024]{1,0:T(8,128)(2,1)S(1)} %get-tuple-element.13.refs_0_, bf16[128,1024]{1,0:T(8,128)(2,1)S(1)} %collective-permute-done.refs_1_, ...), custom_call_target="tpu_custom_call" | custom-call | flops 1500000000 | bytes 1000000 | tf_op jit(solution)/shard_map/pallas_call | solution.py:40
  20.0 1.5 %collective-permute-start.3 = (bf16[128,512]{1,0:T(8,128)(2,1)S(1)}, bf16[128,512]{1,0:T(8,128)(2,1)S(1)}, u32[]{:S(2)}, u32[]{:S(2)}) collective-permute-start(bf16[128,512]{1,0:T(8,128)(2,1)S(1)} %get-tuple-element.18), channel_id=1, source_target_pairs={{0,1},{1,0},{2,3},{3,2},{4,5},{5,4},{6,7},{7,6},{8,9},{9,8},{10,11... | collective-permute-start | bytes 393224 | tf_op jit(solution)/shard_map/ppermute | solution.py:153
  21.5 0.5 %collective-permute-start.4 = (bf16[128,512]{1,0:T(8,128)(2,1)S(1)}, bf16[128,512]{1,0:T(8,128)(2,1)S(1)}, u32[]{:S(2)}, u32[]{:S(2)}) collective-permute-start(bf16[128,512]{1,0:T(8,128)(2,1)S(1)} %get-tuple-element.19), channel_id=1, source_target_pairs={{0,2},{1,3},{2,0},{3,1},{4,6},{5,7},{6,4},{7,5},{8,10},{9,11},{10,... | collective-permute-start | bytes 393224 | tf_op jit(solution)/shard_map/ppermute | solution.py:153
  22.1 1.5 %collective-permute-start.5 = (bf16[128,512]{1,0:T(8,128)(2,1)S(1)}, bf16[128,512]{1,0:T(8,128)(2,1)S(1)}, u32[]{:S(2)}, u32[]{:S(2)}) collective-permute-start(bf16[128,512]{1,0:T(8,128)(2,1)S(1)} %get-tuple-element.20), channel_id=1, source_target_pairs={{0,3},{1,2},{2,1},{3,0},{4,7},{5,6},{6,5},{7,4},{8,11},{9,10},{10,... | collective-permute-start | bytes 393224 | tf_op jit(solution)/shard_map/ppermute | solution.py:153
  23.6 0.8 %collective-permute-done.6.refs_5_ = bf16[128,512]{1,0:T(8,128)(2,1)S(1)} collective-permute-done((bf16[128,512]{1,0:T(8,128)(2,1)S(1)}, bf16[128,512]{1,0:T(8,128)(2,1)S(1)}, u32[]{:S(2)}, u32[]{:S(2)}) %collective-permute-start.6) | collective-permute-done | bytes 131104 | tf_op jit(solution)/shard_map/ppermute | solution.py:153
  25.5 1.4 %collective-permute-done.9 = bf16[4,128,512]{2,1,0:T(8,128)(2,1)S(1)} collective-permute-done((bf16[4,128,512]{2,1,0:T(8,128)(2,1)S(1)}, bf16[4,128,512]{2,1,0:T(8,128)(2,1)S(1)}, u32[]{:S(2)}, u32[]{:S(2)}) %collective-permute-start.9) | collective-permute-done | bytes 524320 | tf_op jit(solution)/shard_map/ppermute | solution.py:153
  27.1 3.2 %collective-permute-start.10 = (bf16[128,512]{1,0:T(8,128)(2,1)S(1)}, bf16[128,512]{1,0:T(8,128)(2,1)S(1)}, u32[]{:S(2)}, u32[]{:S(2)}) collective-permute-start(bf16[128,512]{1,0:T(8,128)(2,1)S(1)} %get-tuple-element.22), channel_id=1, source_target_pairs={{0,16},{4,20},{8,24},{12,28},{16,0},{20,4},{24,8},{28,12},{1,17},{... | collective-permute-start | bytes 393224 | tf_op jit(solution)/shard_map/ppermute | solution.py:153
  30.2 1.3 %collective-permute-start.12 = (bf16[128,512]{1,0:T(8,128)(2,1)S(1)}, bf16[128,512]{1,0:T(8,128)(2,1)S(1)}, u32[]{:S(2)}, u32[]{:S(2)}) collective-permute-start(bf16[128,512]{1,0:T(8,128)(2,1)S(1)} %get-tuple-element.23), channel_id=1, source_target_pairs={{0,24},{4,28},{8,16},{12,20},{16,8},{20,12},{24,0},{28,4},{1,25},{... | collective-permute-start | bytes 393224 | tf_op jit(solution)/shard_map/ppermute | solution.py:153
  31.9 1.9 %shard_map.71 = bf16[128,512]{1,0:T(8,128)(2,1)} custom-call(bf16[128,4096]{1,0:T(8,128)(2,1)S(1)} %copy-done.3, bf16[128,4096]{1,0:T(8,128)(2,1)S(1)} %copy-done.5, f32[128,4096]{1,0:T(8,128)S(1)} %copy-done.8, f32[128,512]{1,0:T(8,128)S(1)} %get-tuple-element.17.rest_0_.refs_8_, bf16[128,512]{1,0:T(8,128)(2,1)S(1)} %collective-permute-done.3.rest_1_, ...), custom_call_target="tpu_custom_call" | custom-call | flops 2500000000 | bytes 1000000 | tf_op jit(solution)/shard_map/pallas_call | solution.py:40
  33.7 6.4 %collective-permute-done.10 = bf16[128,512]{1,0:T(8,128)(2,1)S(1)} collective-permute-done((bf16[128,512]{1,0:T(8,128)(2,1)S(1)}, bf16[128,512]{1,0:T(8,128)(2,1)S(1)}, u32[]{:S(2)}, u32[]{:S(2)}) %collective-permute-start.10) | collective-permute-done | bytes 131104 | tf_op jit(solution)/shard_map/ppermute | solution.py:153
  40.2 0.9 %collective-permute-done.11 = bf16[128,512]{1,0:T(8,128)(2,1)S(1)} collective-permute-done((bf16[128,512]{1,0:T(8,128)(2,1)S(1)}, bf16[128,512]{1,0:T(8,128)(2,1)S(1)}, u32[]{:S(2)}, u32[]{:S(2)}) %collective-permute-start.11) | collective-permute-done | bytes 131104 | tf_op jit(solution)/shard_map/ppermute | solution.py:153
  41.0 0.8 %fusion.2 = f32[128,512]{1,0:T(8,128)} fusion(bf16[128,512]{1,0:T(8,128)(2,1)S(1)} %collective-permute-done.12, bf16[128,512]{1,0:T(8,128)(2,1)S(1)} %collective-permute-done.11, bf16[128,512]{1,0:T(8,128)(2,1)S(1)} %collective-permute-done.10, f32[4,128,512]{2,1,0:T(8,128)S(1)} %convert_add_fusion, s32[]{:T(128)S(6)} %select_n.19), kind=kLoop, calls=%fused_computation.4 | loop fusion | flops 458752 | bytes 917508 | tf_op jit(solution)/shard_map/div | solution.py:187
  (29 shorter events, 2.0 us)
Async XLA Ops:
  0.6 1.2 %copy-start = (bf16[128,4096]{1,0:T(8,128)(2,1)S(1)}, bf16[128,4096]{1,0:T(8,128)(2,1)}, u32[]{:S(2)}) copy-start(bf16[128,4096]{1,0:T(8,128)(2,1)} %source_ref.1) | copy-start | bytes 3145732
  2.0 14.3 %collective-permute-start = (bf16[128,1024]{1,0:T(8,128)(2,1)S(1)}, bf16[128,1024]{1,0:T(8,128)(2,1)S(1)}, u32[]{:S(2)}, u32[]{:S(2)}) collective-permute-start(bf16[128,1024]{1,0:T(8,128)(2,1)S(1)} %get-tuple-element.14), channel_id=1, source_target_pairs={{0,3},{1,2},{2,1},{3,0},{4,7},{5,6},{6,5},{7,4},{8,11},{9,10},{10,... | collective-permute-start | bytes 786440 | tf_op jit(solution)/shard_map/ppermute | solution.py:153
  5.9 12.0 %collective-permute-start.1 = (bf16[128,1024]{1,0:T(8,128)(2,1)S(1)}, bf16[128,1024]{1,0:T(8,128)(2,1)S(1)}, u32[]{:S(2)}, u32[]{:S(2)}) collective-permute-start(bf16[128,1024]{1,0:T(8,128)(2,1)S(1)} %get-tuple-element.15), channel_id=1, source_target_pairs={{0,2},{1,3},{2,0},{3,1},{4,6},{5,7},{6,4},{7,5},{8,10},{9,11},{10,... | collective-permute-start | bytes 786440 | tf_op jit(solution)/shard_map/ppermute | solution.py:153
  6.4 12.9 %copy-start.1 = (bf16[1024,512]{1,0:T(8,128)(2,1)S(1)}, bf16[1024,512]{1,0:T(8,128)(2,1)}, u32[]{:S(2)}) copy-start(bf16[1024,512]{1,0:T(8,128)(2,1)} %refs_4_.1) | copy-start | bytes 3145732
  6.4 12.9 %collective-permute-start.2 = (bf16[128,1024]{1,0:T(8,128)(2,1)S(1)}, bf16[128,1024]{1,0:T(8,128)(2,1)S(1)}, u32[]{:S(2)}, u32[]{:S(2)}) collective-permute-start(bf16[128,1024]{1,0:T(8,128)(2,1)S(1)} %get-tuple-element.16), channel_id=1, source_target_pairs={{0,1},{1,0},{2,3},{3,2},{4,5},{5,4},{6,7},{7,6},{8,9},{9,8},{10,11... | collective-permute-start | bytes 786440 | tf_op jit(solution)/shard_map/ppermute | solution.py:153
  6.6 1.3 %copy-start.2 = (bf16[128,4096]{1,0:T(8,128)(2,1)S(1)}, bf16[128,4096]{1,0:T(8,128)(2,1)}, u32[]{:S(2)}) copy-start(bf16[128,4096]{1,0:T(8,128)(2,1)} %q_ref.3) | copy-start | bytes 3145732
  7.9 1.2 %copy-start.4 = (bf16[128,4096]{1,0:T(8,128)(2,1)S(1)}, bf16[128,4096]{1,0:T(8,128)(2,1)}, u32[]{:S(2)}) copy-start(bf16[128,4096]{1,0:T(8,128)(2,1)} %g_ref.3) | copy-start | bytes 3145732
  9.1 0.9 %copy-start.6 = (bf16[128,512]{1,0:T(8,128)(2,1)S(1)}, bf16[128,512]{1,0:T(8,128)(2,1)}, u32[]{:S(2)}) copy-start(bf16[128,512]{1,0:T(8,128)(2,1)} %k_ref.1) | copy-start | bytes 393220
  11.6 1.3 %copy-start.7 = (f32[128,4096]{1,0:T(8,128)}, f32[128,4096]{1,0:T(8,128)S(1)}, u32[]{:S(2)}) copy-start(f32[128,4096]{1,0:T(8,128)S(1)} %get-tuple-element.12.p_ref) | copy-start | bytes 6291460
  13.0 9.2 %collective-permute-start.8 = (bf16[128,512]{1,0:T(8,128)(2,1)S(1)}, bf16[128,512]{1,0:T(8,128)(2,1)S(1)}, u32[]{:S(2)}, u32[]{:S(2)}) collective-permute-start(bf16[128,512]{1,0:T(8,128)(2,1)S(1)} %get-tuple-element.21.refs_4_), channel_id=1, source_target_pairs={{0,1},{1,0},{2,3},{3,2},{4,5},{5,4},{6,7},{7,6},{8,9},{9,8},{10,11... | collective-permute-start | bytes 393224 | tf_op jit(solution)/shard_map/ppermute | solution.py:153
  14.8 8.8 %collective-permute-start.7 = (bf16[128,512]{1,0:T(8,128)(2,1)S(1)}, bf16[128,512]{1,0:T(8,128)(2,1)S(1)}, u32[]{:S(2)}, u32[]{:S(2)}) collective-permute-start(bf16[128,512]{1,0:T(8,128)(2,1)S(1)} %get-tuple-element.21.refs_4_), channel_id=1, source_target_pairs={{0,2},{1,3},{2,0},{3,1},{4,6},{5,7},{6,4},{7,5},{8,10},{9,11},{10,... | collective-permute-start | bytes 393224 | tf_op jit(solution)/shard_map/ppermute | solution.py:153
  16.3 8.1 %collective-permute-start.6 = (bf16[128,512]{1,0:T(8,128)(2,1)S(1)}, bf16[128,512]{1,0:T(8,128)(2,1)S(1)}, u32[]{:S(2)}, u32[]{:S(2)}) collective-permute-start(bf16[128,512]{1,0:T(8,128)(2,1)S(1)} %get-tuple-element.21.refs_4_), channel_id=1, source_target_pairs={{0,3},{1,2},{2,1},{3,0},{4,7},{5,6},{6,5},{7,4},{8,11},{9,10},{10,... | collective-permute-start | bytes 393224 | tf_op jit(solution)/shard_map/ppermute | solution.py:153
  20.0 11.6 %collective-permute-start.3 = (bf16[128,512]{1,0:T(8,128)(2,1)S(1)}, bf16[128,512]{1,0:T(8,128)(2,1)S(1)}, u32[]{:S(2)}, u32[]{:S(2)}) collective-permute-start(bf16[128,512]{1,0:T(8,128)(2,1)S(1)} %get-tuple-element.18), channel_id=1, source_target_pairs={{0,1},{1,0},{2,3},{3,2},{4,5},{5,4},{6,7},{7,6},{8,9},{9,8},{10,11... | collective-permute-start | bytes 393224 | tf_op jit(solution)/shard_map/ppermute | solution.py:153
  21.5 10.3 %collective-permute-start.4 = (bf16[128,512]{1,0:T(8,128)(2,1)S(1)}, bf16[128,512]{1,0:T(8,128)(2,1)S(1)}, u32[]{:S(2)}, u32[]{:S(2)}) collective-permute-start(bf16[128,512]{1,0:T(8,128)(2,1)S(1)} %get-tuple-element.19), channel_id=1, source_target_pairs={{0,2},{1,3},{2,0},{3,1},{4,6},{5,7},{6,4},{7,5},{8,10},{9,11},{10,... | collective-permute-start | bytes 393224 | tf_op jit(solution)/shard_map/ppermute | solution.py:153
  22.1 9.7 %collective-permute-start.5 = (bf16[128,512]{1,0:T(8,128)(2,1)S(1)}, bf16[128,512]{1,0:T(8,128)(2,1)S(1)}, u32[]{:S(2)}, u32[]{:S(2)}) collective-permute-start(bf16[128,512]{1,0:T(8,128)(2,1)S(1)} %get-tuple-element.20), channel_id=1, source_target_pairs={{0,3},{1,2},{2,1},{3,0},{4,7},{5,6},{6,5},{7,4},{8,11},{9,10},{10,... | collective-permute-start | bytes 393224 | tf_op jit(solution)/shard_map/ppermute | solution.py:153
  24.8 2.0 %collective-permute-start.9 = (bf16[4,128,512]{2,1,0:T(8,128)(2,1)S(1)}, bf16[4,128,512]{2,1,0:T(8,128)(2,1)S(1)}, u32[]{:S(2)}, u32[]{:S(2)}) collective-permute-start(bf16[4,128,512]{2,1,0:T(8,128)(2,1)S(1)} %shard_map.73), channel_id=1, source_target_pairs={{0,4},{4,0},{8,12},{12,8},{16,20},{20,16},{24,28},{28,24},{1,5},{5... | collective-permute-start | bytes 1572872 | tf_op jit(solution)/shard_map/ppermute | solution.py:153
  24.9 6.9 %copy-start.8 = (f32[128,4096]{1,0:T(8,128)S(1)}, f32[128,4096]{1,0:T(8,128)}, u32[]{:S(2)}) copy-start(f32[128,4096]{1,0:T(8,128)} %copy-done.7) | copy-start | bytes 6291460
  25.4 6.4 %copy-start.3 = (bf16[128,4096]{1,0:T(8,128)(2,1)S(1)}, bf16[128,4096]{1,0:T(8,128)(2,1)}, u32[]{:S(2)}) copy-start(bf16[128,4096]{1,0:T(8,128)(2,1)} %q_ref.3) | copy-start | bytes 3145732
  25.4 6.4 %copy-start.5 = (bf16[128,4096]{1,0:T(8,128)(2,1)S(1)}, bf16[128,4096]{1,0:T(8,128)(2,1)}, u32[]{:S(2)}) copy-start(bf16[128,4096]{1,0:T(8,128)(2,1)} %g_ref.3) | copy-start | bytes 3145732
  27.1 13.1 %collective-permute-start.10 = (bf16[128,512]{1,0:T(8,128)(2,1)S(1)}, bf16[128,512]{1,0:T(8,128)(2,1)S(1)}, u32[]{:S(2)}, u32[]{:S(2)}) collective-permute-start(bf16[128,512]{1,0:T(8,128)(2,1)S(1)} %get-tuple-element.22), channel_id=1, source_target_pairs={{0,16},{4,20},{8,24},{12,28},{16,0},{20,4},{24,8},{28,12},{1,17},{... | collective-permute-start | bytes 393224 | tf_op jit(solution)/shard_map/ppermute | solution.py:153
  30.2 10.0 %collective-permute-start.12 = (bf16[128,512]{1,0:T(8,128)(2,1)S(1)}, bf16[128,512]{1,0:T(8,128)(2,1)S(1)}, u32[]{:S(2)}, u32[]{:S(2)}) collective-permute-start(bf16[128,512]{1,0:T(8,128)(2,1)S(1)} %get-tuple-element.23), channel_id=1, source_target_pairs={{0,24},{4,28},{8,16},{12,20},{16,8},{20,12},{24,0},{28,4},{1,25},{... | collective-permute-start | bytes 393224 | tf_op jit(solution)/shard_map/ppermute | solution.py:153
  31.6 9.5 %collective-permute-start.11 = (bf16[128,512]{1,0:T(8,128)(2,1)S(1)}, bf16[128,512]{1,0:T(8,128)(2,1)S(1)}, u32[]{:S(2)}, u32[]{:S(2)}) collective-permute-start(bf16[128,512]{1,0:T(8,128)(2,1)S(1)} %get-tuple-element.24), channel_id=1, source_target_pairs={{0,8},{4,12},{8,0},{12,4},{16,24},{20,28},{24,16},{28,20},{1,9},{5... | collective-permute-start | bytes 393224 | tf_op jit(solution)/shard_map/ppermute | solution.py:153

commit v4 on v3

--- a/solution.py
+++ b/solution.py
@@ -115,37 +115,50 @@
     return call(key_kernel, outs, 2_500_000_000, (queries, gradient, attention, *values))[0]
 
 
-def values_kernel(*refs):
-    n = len(refs) // 2
+def values_kernel(n, *refs):
     weights = refs[n][...]
-    for source, out in zip(refs[:n], refs[n + 1 :]):
+    for source, out in zip(refs[:n], refs[-n:]):
         out[...] = dot(source[...], weights).astype(out.dtype)
 
 
-def values_call(blocks, weights):
+def values_call(blocks, weights, after=()):
     n = len(blocks)
     shape = (blocks[0].shape[0], weights.shape[1])
     outs = [struct(shape, jnp.float32 if i == 0 else jnp.bfloat16) for i in range(n)]
-    return call(values_kernel, outs, 1500000000, (*blocks, weights))
-
-
-def weight_kernel(n, other, owners, *refs):
+    kernel = functools.partial(values_kernel, n)
+    in_specs = [VMEM] * (n + 1) + [pl.BlockSpec(memory_space=pl.ANY)] * len(after)
+    return call(kernel, outs, 1_500_000_000, (*blocks, weights, *after), in_specs)
+
+
+def weight_kernel(n, other, distances, *refs):
     blocks, d_values, out_ref = refs[:n], refs[n : 2 * n], refs[-1]
-    chips, rows, width = out_ref.shape
-    core = (lax.axis_index("dp") + other) % 2
-    columns = [pl.ds(pl.multiple_of((2 * i + core) * rows, rows), rows) for i in range(chips)]
+    _, rows, width = out_ref.shape
+    owner = lax.axis_index("dp")
+    core, chip = (owner + other) % 2, owner // 2
+    starts = [(2 * (chip ^ k) + core) * rows for k in distances]
+    columns = [pl.ds(pl.multiple_of(start, rows), rows) for start in starts]
     source = jnp.concatenate(
         [jnp.concatenate([ref[:, c] for c in columns], axis=1) for ref in blocks], axis=0
     )
     product = dot_tn(source, jnp.concatenate([ref[...] for ref in d_values], axis=0))
-    out_ref[...] = product.reshape(chips, rows, width).astype(out_ref.dtype)
-
-
-def weight_call(blocks, d_values, other, owners, dtype, after=(), flops=1_000_000_000):
-    shape = (owners // 2, blocks[0].shape[1] // owners, d_values[0].shape[1])
-    kernel = functools.partial(weight_kernel, len(blocks), other, owners)
+    out_ref[...] = product.reshape(len(distances), rows, width).astype(out_ref.dtype)
+
+
+def weight_call(blocks, d_values, other, owners, distances, after=(), flops=500_000_000):
+    dtype = jnp.bfloat16 if other else jnp.float32
+    shape = (len(distances), blocks[0].shape[1] // owners, d_values[0].shape[1])
+    kernel = functools.partial(weight_kernel, len(blocks), other, distances)
     in_specs = [VMEM] * (2 * len(blocks)) + [pl.BlockSpec(memory_space=pl.ANY)] * len(after)
     return call(kernel, [struct(shape, dtype)], flops, (*blocks, *d_values, *after), in_specs)[0]
+
+
+def mark_kernel(*refs):
+    refs[-1][...] = jnp.zeros_like(refs[-1])
+
+
+def mark(arrays):
+    in_specs = [pl.BlockSpec(memory_space=pl.ANY)] * len(arrays)
+    return call(mark_kernel, [struct((8, 128), jnp.float32)], 100_000_000, arrays, in_specs)[0]
 
 
 def swap(array, axis, distance):
@@ -155,7 +168,6 @@
 
 def per_device(inputs, queries, keys, attention_gradient, value_matrix):
     nodes, owners = lax.axis_size("node"), lax.axis_size("dp")
-    owner = lax.axis_index("dp")
     width = inputs.shape[1] // nodes
 
     packed = pack_call(inputs, nodes)
@@ -163,27 +175,41 @@
     order = [0, *range(nodes - 1, 0, -1)]
     d_values, attention = softmax_call(queries, keys, attention_gradient)
     all_d_values = [d_values] + [swap(d_values, "node", k) for k in range(1, nodes)]
-    parts = values_call([blocks[k] for k in order], value_matrix)
+
+    rows = width // owners
+    if rows % 16 or owners % 4:
+        parts = values_call([blocks[k] for k in order], value_matrix, ())
+        parts = [parts[order.index(k)] for k in range(nodes)]
+        values = [parts[0]] + [swap(parts[k], "node", k) for k in range(1, nodes)]
+        key_gradient = key_call(queries, attention_gradient, attention, values)
+        local = dot_tn(jnp.concatenate(blocks, axis=0), jnp.concatenate(all_d_values, axis=0))
+        owned = lax.psum_scatter(local, "dp", scatter_dimension=0, tiled=True)
+        return key_gradient, owned / (owners * nodes)
+    chips = owners // 2
+    ordered = [blocks[k] for k in order], [all_d_values[k] for k in order]
+    low, wide = jnp.bfloat16, jnp.float32
+    halves = tuple(range(chips // 2, chips)), tuple(range(chips // 2))
+    tick = mark(blocks[1:])
+    pairs, keeps = {}, ()
+    for distances in halves:
+        send = weight_call(*ordered, 1, owners, distances, (tick, *keeps))
+        keep = weight_call(*ordered, 0, owners, distances, (), 500_000_000)
+        keeps = (keep,)
+        pair = keep + swap(send, "dp", 1).astype(wide)
+        pairs.update((k, pair[i]) for i, k in enumerate(distances))
+
+    parts = values_call([blocks[k] for k in order], value_matrix, (pairs[chips // 2],))
     parts = [parts[order.index(k)] for k in range(nodes)]
     values = [parts[0]] + [swap(parts[k], "node", k) for k in range(1, nodes)]
     key_gradient = key_call(queries, attention_gradient, attention, values)
-
-    rows = width // owners
-    if rows % 16 or owners % 2:
-        local = dot_tn(jnp.concatenate(blocks, axis=0), jnp.concatenate(all_d_values, axis=0))
-        owned = lax.psum_scatter(local, "dp", scatter_dimension=0, tiled=True)
-        return key_gradient, owned / (owners * nodes)
-    chip, chips = owner // 2, owners // 2
-    send = weight_call([blocks[k] for k in order], [all_d_values[k] for k in order], 1, owners, jnp.bfloat16, (parts[0],))
-    keep = weight_call([blocks[k] for k in order], [all_d_values[k] for k in order], 0, owners, jnp.float32, (), 6000000000)
-    pair = keep + swap(send, "dp", 1).astype(jnp.float32)
-
-    def chip_rows(other):
-        return lax.dynamic_index_in_dim(pair, other, axis=0, keepdims=False)
-
-    owned = chip_rows(chip)
-    for k in sorted(range(1, chips), key=lambda k: (k == chips - 1, k % 2)):
-        owned += swap(chip_rows(chip ^ k).astype(jnp.bfloat16), "dp", 2 * k).astype(jnp.float32)
+    owned = pairs[0]
+    if chips == 4:
+        passed = pairs[2] + swap(pairs[3].astype(low), "dp", 2).astype(wide)
+        owned += swap(pairs[1].astype(low), "dp", 2).astype(wide)
+        owned += swap(passed.astype(low), "dp", 4).astype(wide)
+    else:
+        for k in range(1, chips):
+            owned += swap(pairs[k].astype(low), "dp", 2 * k).astype(wide)
     return key_gradient, owned / (owners * nodes)
 
 

time: 42.3 us -> 40.7 us (0.962)
  waiting for transfers between devices: 12.3 us -> 10.1 us
  starting transfers between devices: 16.4 us -> 18.3 us
  local copies, waits for them, and re-layouts: 6.05 us -> 4.65 us
    ppermute x13 -> x14, waiting for transfers between devices: 12.3 us -> 10.1 us  [swap(): return lax.ppermute(array, axis, [(i, i ^ distance) for i in range(size)])]
    ppermute x13 -> x14, starting transfers between devices: 16.4 us -> 18.3 us  [swap(): return lax.ppermute(array, axis, [(i, i ^ distance) for i in range(size)])]
    unnamed x18 -> x14, local copies, waits for them, and re-layouts: 5.99 us -> 4.59 us
    pallas_call x6 -> x9, Pallas kernels: 5.32 us -> 5.7 us  [call(): pl.pallas_call(kernel, in_specs=in_specs or [VMEM] * len(arguments), out_...]
  transfers between devices with their start and end apart: 13 -> 14, of which waited for: 6 -> 6; matrix products, arithmetic and copies ran while one was open for 1% -> 1% of each run, Pallas kernels for 12% -> 13%
where the time goes in v4:
time: 40.7 us; the launch traced here: 40.4 us
  starting transfers between devices  18.3 us (45%)
  waiting for transfers between devices  10.1 us (25%)
  Pallas kernels  5.7 us (14%)
  local copies, waits for them, and re-layouts  4.65 us (11%)
  other arithmetic  0.93 us (2%)
  between operations  0.8 us (2%)
    ppermute x14, starting transfers between devices, swap(): return lax.ppermute(array, axis, [(i, i ^ distance) for i in range(size)])  18.3 us
    ppermute x14, waiting for transfers between devices, swap(): return lax.ppermute(array, axis, [(i, i ^ distance) for i in range(size)])  10.1 us
    pallas_call x9, Pallas kernels, call(): pl.pallas_call(kernel, in_specs=in_specs or [VMEM] * len(arguments), out_...  5.7 us
    unnamed x14, local copies, waits for them, and re-layouts  4.59 us
  transfers between devices with their start and end apart: 14, of which 6 were waited for; matrix products, arithmetic and copies ran while one was open for 1% of the time, Pallas kernels for 13%

profile of v4, /device:TPU:0, one launch (start us, length us, event | category | flops | bytes accessed | tf_op | source)
XLA Modules:
  0.0 40.4 jit_solution(714942113050948463)
XLA Ops:
  0.6 1.2 %copy-done = bf16[128,4096]{1,0:T(8,128)(2,1)S(1)} copy-done((bf16[128,4096]{1,0:T(8,128)(2,1)S(1)}, bf16[128,4096]{1,0:T(8,128)(2,1)}, u32[]{:S(2)}) %copy-start) | copy-done | bytes 1048600
  2.0 4.0 %collective-permute-start = (bf16[128,1024]{1,0:T(8,128)(2,1)S(1)}, bf16[128,1024]{1,0:T(8,128)(2,1)S(1)}, u32[]{:S(2)}, u32[]{:S(2)}) collective-permute-start(bf16[128,1024]{1,0:T(8,128)(2,1)S(1)} %get-tuple-element.14), channel_id=1, source_target_pairs={{0,3},{1,2},{2,1},{3,0},{4,7},{5,6},{6,5},{7,4},{8,11},{9,10},{10,... | collective-permute-start | bytes 786440 | tf_op jit(solution)/shard_map/ppermute | solution.py:166
  5.9 0.5 %collective-permute-start.1 = (bf16[128,1024]{1,0:T(8,128)(2,1)S(1)}, bf16[128,1024]{1,0:T(8,128)(2,1)S(1)}, u32[]{:S(2)}, u32[]{:S(2)}) collective-permute-start(bf16[128,1024]{1,0:T(8,128)(2,1)S(1)} %get-tuple-element.15), channel_id=1, source_target_pairs={{0,2},{1,3},{2,0},{3,1},{4,6},{5,7},{6,4},{7,5},{8,10},{9,11},{10,... | collective-permute-start | bytes 786440 | tf_op jit(solution)/shard_map/ppermute | solution.py:166
  6.6 1.2 %copy-done.2 = bf16[128,4096]{1,0:T(8,128)(2,1)S(1)} copy-done((bf16[128,4096]{1,0:T(8,128)(2,1)S(1)}, bf16[128,4096]{1,0:T(8,128)(2,1)}, u32[]{:S(2)}) %copy-start.2) | copy-done | bytes 1048600
  7.8 1.2 %copy-done.4 = bf16[128,4096]{1,0:T(8,128)(2,1)S(1)} copy-done((bf16[128,4096]{1,0:T(8,128)(2,1)S(1)}, bf16[128,4096]{1,0:T(8,128)(2,1)}, u32[]{:S(2)}) %copy-start.4) | copy-done | bytes 1048600
  9.0 0.9 %copy-done.6 = bf16[128,512]{1,0:T(8,128)(2,1)S(1)} copy-done((bf16[128,512]{1,0:T(8,128)(2,1)S(1)}, bf16[128,512]{1,0:T(8,128)(2,1)}, u32[]{:S(2)}) %copy-start.6) | copy-done | bytes 131096
  9.9 1.6 %shard_map.68 = (bf16[128,512]{1,0:T(8,128)(2,1)S(1)}, f32[128,4096]{1,0:T(8,128)S(1)}) custom-call(bf16[128,4096]{1,0:T(8,128)(2,1)S(1)} %copy-done.2, bf16[128,512]{1,0:T(8,128)(2,1)S(1)} %copy-done.6, bf16[128,4096]{1,0:T(8,128)(2,1)S(1)} %copy-done.4), custom_call_target="tpu_custom_call" | custom-call | flops 3000000000 | bytes 1000000 | tf_op jit(solution)/shard_map/pallas_call | solution.py:40
  11.5 2.0 %collective-permute-start.5 = (bf16[128,512]{1,0:T(8,128)(2,1)S(1)}, bf16[128,512]{1,0:T(8,128)(2,1)S(1)}, u32[]{:S(2)}, u32[]{:S(2)}) collective-permute-start(bf16[128,512]{1,0:T(8,128)(2,1)S(1)} %get-tuple-element.17.refs_4_), channel_id=1, source_target_pairs={{0,1},{1,0},{2,3},{3,2},{4,5},{5,4},{6,7},{7,6},{8,9},{9,8},{10,11... | collective-permute-start | bytes 393224 | tf_op jit(solution)/shard_map/ppermute | solution.py:166
  13.5 1.5 %collective-permute-start.4 = (bf16[128,512]{1,0:T(8,128)(2,1)S(1)}, bf16[128,512]{1,0:T(8,128)(2,1)S(1)}, u32[]{:S(2)}, u32[]{:S(2)}) collective-permute-start(bf16[128,512]{1,0:T(8,128)(2,1)S(1)} %get-tuple-element.17.refs_4_), channel_id=1, source_target_pairs={{0,2},{1,3},{2,0},{3,1},{4,6},{5,7},{6,4},{7,5},{8,10},{9,11},{10,... | collective-permute-start | bytes 393224 | tf_op jit(solution)/shard_map/ppermute | solution.py:166
  15.0 1.0 %collective-permute-start.3 = (bf16[128,512]{1,0:T(8,128)(2,1)S(1)}, bf16[128,512]{1,0:T(8,128)(2,1)S(1)}, u32[]{:S(2)}, u32[]{:S(2)}) collective-permute-start(bf16[128,512]{1,0:T(8,128)(2,1)S(1)} %get-tuple-element.17.refs_4_), channel_id=1, source_target_pairs={{0,3},{1,2},{2,1},{3,0},{4,7},{5,6},{6,5},{7,4},{8,11},{9,10},{10,... | collective-permute-start | bytes 393224 | tf_op jit(solution)/shard_map/ppermute | solution.py:166
  16.0 1.9 %collective-permute-done.1.refs_2_.refs_1_ = bf16[128,1024]{1,0:T(8,128)(2,1)S(1)} collective-permute-done((bf16[128,1024]{1,0:T(8,128)(2,1)S(1)}, bf16[128,1024]{1,0:T(8,128)(2,1)S(1)}, u32[]{:S(2)}, u32[]{:S(2)}) %collective-permute-start.1) | collective-permute-done | bytes 262176 | tf_op jit(solution)/shard_map/ppermute | solution.py:166
  18.0 1.3 %collective-permute-done.2.refs_3_.refs_0_ = bf16[128,1024]{1,0:T(8,128)(2,1)S(1)} collective-permute-done((bf16[128,1024]{1,0:T(8,128)(2,1)S(1)}, bf16[128,1024]{1,0:T(8,128)(2,1)S(1)}, u32[]{:S(2)}, u32[]{:S(2)}) %collective-permute-start.2) | collective-permute-done | bytes 262176 | tf_op jit(solution)/shard_map/ppermute | solution.py:166
  19.3 2.8 %collective-permute-done.5.refs_7_ = bf16[128,512]{1,0:T(8,128)(2,1)S(1)} collective-permute-done((bf16[128,512]{1,0:T(8,128)(2,1)S(1)}, bf16[128,512]{1,0:T(8,128)(2,1)S(1)}, u32[]{:S(2)}, u32[]{:S(2)}) %collective-permute-start.5) | collective-permute-done | bytes 131104 | tf_op jit(solution)/shard_map/ppermute | solution.py:166
  22.1 1.4 %collective-permute-done.3.refs_5_ = bf16[128,512]{1,0:T(8,128)(2,1)S(1)} collective-permute-done((bf16[128,512]{1,0:T(8,128)(2,1)S(1)}, bf16[128,512]{1,0:T(8,128)(2,1)S(1)}, u32[]{:S(2)}, u32[]{:S(2)}) %collective-permute-start.3) | collective-permute-done | bytes 131104 | tf_op jit(solution)/shard_map/ppermute | solution.py:166
  24.7 0.6 %collective-permute-start.10 = (bf16[2,128,512]{2,1,0:T(8,128)(2,1)S(1)}, bf16[2,128,512]{2,1,0:T(8,128)(2,1)S(1)}, u32[]{:S(2)}, u32[]{:S(2)}) collective-permute-start(bf16[2,128,512]{2,1,0:T(8,128)(2,1)S(1)} %shard_map.76), channel_id=1, source_target_pairs={{0,4},{4,0},{8,12},{12,8},{16,20},{20,16},{24,28},{28,24},{1,5},{5... | collective-permute-start | bytes 786440 | tf_op jit(solution)/shard_map/ppermute | solution.py:166
  25.7 1.8 %collective-permute-start.12 = (bf16[128,512]{1,0:T(8,128)(2,1)S(1)}, bf16[128,512]{1,0:T(8,128)(2,1)S(1)}, u32[]{:S(2)}, u32[]{:S(2)}) collective-permute-start(bf16[128,512]{1,0:T(8,128)(2,1)S(1)} %fusion.4), channel_id=1, source_target_pairs={{0,8},{4,12},{8,0},{12,4},{16,24},{20,28},{24,16},{28,20},{1,9},{5... | collective-permute-start | bytes 393224 | tf_op jit(solution)/shard_map/ppermute | solution.py:166
  27.6 0.7 %shard_map.73 = (f32[128,512]{1,0:T(8,128)S(1)}, bf16[128,512]{1,0:T(8,128)(2,1)S(1)}, bf16[128,512]{1,0:T(8,128)(2,1)S(1)}, bf16[128,512]{1,0:T(8,128)(2,1)S(1)}) custom-call(bf16[128,1024]{1,0:T(8,128)(2,1)S(1)} %get-tuple-element.13.refs_0_, bf16[128,1024]{1,0:T(8,128)(2,1)S(1)} %collective-permute-done.refs_1_.refs_2_, ...), custom_call_target="tpu_custom_call" | custom-call | flops 1500000000 | bytes 1000000 | tf_op jit(solution)/shard_map/pallas_call | solution.py:40
  28.3 1.6 %collective-permute-start.7 = (bf16[128,512]{1,0:T(8,128)(2,1)S(1)}, bf16[128,512]{1,0:T(8,128)(2,1)S(1)}, u32[]{:S(2)}, u32[]{:S(2)}) collective-permute-start(bf16[128,512]{1,0:T(8,128)(2,1)S(1)} %get-tuple-element.19), channel_id=1, source_target_pairs={{0,1},{1,0},{2,3},{3,2},{4,5},{5,4},{6,7},{7,6},{8,9},{9,8},{10,11... | collective-permute-start | bytes 393224 | tf_op jit(solution)/shard_map/ppermute | solution.py:166
  29.9 1.5 %collective-permute-start.8 = (bf16[128,512]{1,0:T(8,128)(2,1)S(1)}, bf16[128,512]{1,0:T(8,128)(2,1)S(1)}, u32[]{:S(2)}, u32[]{:S(2)}) collective-permute-start(bf16[128,512]{1,0:T(8,128)(2,1)S(1)} %get-tuple-element.20), channel_id=1, source_target_pairs={{0,2},{1,3},{2,0},{3,1},{4,6},{5,7},{6,4},{7,5},{8,10},{9,11},{10,... | collective-permute-start | bytes 393224 | tf_op jit(solution)/shard_map/ppermute | solution.py:166
  31.4 0.5 %collective-permute-start.9 = (bf16[128,512]{1,0:T(8,128)(2,1)S(1)}, bf16[128,512]{1,0:T(8,128)(2,1)S(1)}, u32[]{:S(2)}, u32[]{:S(2)}) collective-permute-start(bf16[128,512]{1,0:T(8,128)(2,1)S(1)} %get-tuple-element.21), channel_id=1, source_target_pairs={{0,3},{1,2},{2,1},{3,0},{4,7},{5,6},{6,5},{7,4},{8,11},{9,10},{10,... | collective-permute-start | bytes 393224 | tf_op jit(solution)/shard_map/ppermute | solution.py:166
  32.3 2.8 %collective-permute-start.13 = (bf16[128,512]{1,0:T(8,128)(2,1)S(1)}, bf16[128,512]{1,0:T(8,128)(2,1)S(1)}, u32[]{:S(2)}, u32[]{:S(2)}) collective-permute-start(bf16[128,512]{1,0:T(8,128)(2,1)S(1)} %add_convert_fusion), channel_id=1, source_target_pairs={{0,16},{4,20},{8,24},{12,28},{16,0},{20,4},{24,8},{28,12},{1,17},{... | collective-permute-start | bytes 393224 | tf_op jit(solution)/shard_map/ppermute | solution.py:166
  35.2 2.5 %collective-permute-done.8.rest_2_ = bf16[128,512]{1,0:T(8,128)(2,1)S(1)} collective-permute-done((bf16[128,512]{1,0:T(8,128)(2,1)S(1)}, bf16[128,512]{1,0:T(8,128)(2,1)S(1)}, u32[]{:S(2)}, u32[]{:S(2)}) %collective-permute-start.8) | collective-permute-done | bytes 131104 | tf_op jit(solution)/shard_map/ppermute | solution.py:166
  37.7 1.9 %shard_map.74 = bf16[128,512]{1,0:T(8,128)(2,1)} custom-call(bf16[128,4096]{1,0:T(8,128)(2,1)S(1)} %copy-done.3, bf16[128,4096]{1,0:T(8,128)(2,1)S(1)} %copy-done.5, f32[128,4096]{1,0:T(8,128)S(1)} %get-tuple-element.12.p_ref, f32[128,512]{1,0:T(8,128)S(1)} %get-tuple-element.18.rest_0_, bf16[128,512]{1,0:T(8,128)(2,1)S(1)} %collective-permute-done.7.rest_1_, ...), custom_call_target="tpu_custom_call" | custom-call | flops 2500000000 | bytes 1000000 | tf_op jit(solution)/shard_map/pallas_call | solution.py:40
  39.7 0.8 %fusion.2 = f32[128,512]{1,0:T(8,128)} fusion(f32[2,128,512]{2,1,0:T(8,128)S(1)} %convert_add_fusion, bf16[128,512]{1,0:T(8,128)(2,1)S(1)} %collective-permute-done.13, bf16[128,512]{1,0:T(8,128)(2,1)S(1)} %collective-permute-done.11), kind=kLoop, calls=%fused_computation.7 | loop fusion | flops 327680 | bytes 786432 | tf_op jit(solution)/shard_map/div | solution.py:213
  (34 shorter events, 2.4 us)
Async XLA Ops:
  0.6 1.2 %copy-start = (bf16[128,4096]{1,0:T(8,128)(2,1)S(1)}, bf16[128,4096]{1,0:T(8,128)(2,1)}, u32[]{:S(2)}) copy-start(bf16[128,4096]{1,0:T(8,128)(2,1)} %source_ref.1) | copy-start | bytes 3145732
  2.0 13.0 %collective-permute-start = (bf16[128,1024]{1,0:T(8,128)(2,1)S(1)}, bf16[128,1024]{1,0:T(8,128)(2,1)S(1)}, u32[]{:S(2)}, u32[]{:S(2)}) collective-permute-start(bf16[128,1024]{1,0:T(8,128)(2,1)S(1)} %get-tuple-element.14), channel_id=1, source_target_pairs={{0,3},{1,2},{2,1},{3,0},{4,7},{5,6},{6,5},{7,4},{8,11},{9,10},{10,... | collective-permute-start | bytes 786440 | tf_op jit(solution)/shard_map/ppermute | solution.py:166
  5.9 12.0 %collective-permute-start.1 = (bf16[128,1024]{1,0:T(8,128)(2,1)S(1)}, bf16[128,1024]{1,0:T(8,128)(2,1)S(1)}, u32[]{:S(2)}, u32[]{:S(2)}) collective-permute-start(bf16[128,1024]{1,0:T(8,128)(2,1)S(1)} %get-tuple-element.15), channel_id=1, source_target_pairs={{0,2},{1,3},{2,0},{3,1},{4,6},{5,7},{6,4},{7,5},{8,10},{9,11},{10,... | collective-permute-start | bytes 786440 | tf_op jit(solution)/shard_map/ppermute | solution.py:166
  6.4 12.9 %collective-permute-start.2 = (bf16[128,1024]{1,0:T(8,128)(2,1)S(1)}, bf16[128,1024]{1,0:T(8,128)(2,1)S(1)}, u32[]{:S(2)}, u32[]{:S(2)}) collective-permute-start(bf16[128,1024]{1,0:T(8,128)(2,1)S(1)} %get-tuple-element.16), channel_id=1, source_target_pairs={{0,1},{1,0},{2,3},{3,2},{4,5},{5,4},{6,7},{7,6},{8,9},{9,8},{10,11... | collective-permute-start | bytes 786440 | tf_op jit(solution)/shard_map/ppermute | solution.py:166
  6.6 1.2 %copy-start.2 = (bf16[128,4096]{1,0:T(8,128)(2,1)S(1)}, bf16[128,4096]{1,0:T(8,128)(2,1)}, u32[]{:S(2)}) copy-start(bf16[128,4096]{1,0:T(8,128)(2,1)} %q_ref.3) | copy-start | bytes 3145732
  7.8 1.2 %copy-start.4 = (bf16[128,4096]{1,0:T(8,128)(2,1)S(1)}, bf16[128,4096]{1,0:T(8,128)(2,1)}, u32[]{:S(2)}) copy-start(bf16[128,4096]{1,0:T(8,128)(2,1)} %g_ref.3) | copy-start | bytes 3145732
  9.0 0.9 %copy-start.6 = (bf16[128,512]{1,0:T(8,128)(2,1)S(1)}, bf16[128,512]{1,0:T(8,128)(2,1)}, u32[]{:S(2)}) copy-start(bf16[128,512]{1,0:T(8,128)(2,1)} %k_ref.1) | copy-start | bytes 393220
  11.5 10.6 %collective-permute-start.5 = (bf16[128,512]{1,0:T(8,128)(2,1)S(1)}, bf16[128,512]{1,0:T(8,128)(2,1)S(1)}, u32[]{:S(2)}, u32[]{:S(2)}) collective-permute-start(bf16[128,512]{1,0:T(8,128)(2,1)S(1)} %get-tuple-element.17.refs_4_), channel_id=1, source_target_pairs={{0,1},{1,0},{2,3},{3,2},{4,5},{5,4},{6,7},{7,6},{8,9},{9,8},{10,11... | collective-permute-start | bytes 393224 | tf_op jit(solution)/shard_map/ppermute | solution.py:166
  13.5 8.6 %collective-permute-start.4 = (bf16[128,512]{1,0:T(8,128)(2,1)S(1)}, bf16[128,512]{1,0:T(8,128)(2,1)S(1)}, u32[]{:S(2)}, u32[]{:S(2)}) collective-permute-start(bf16[128,512]{1,0:T(8,128)(2,1)S(1)} %get-tuple-element.17.refs_4_), channel_id=1, source_target_pairs={{0,2},{1,3},{2,0},{3,1},{4,6},{5,7},{6,4},{7,5},{8,10},{9,11},{10,... | collective-permute-start | bytes 393224 | tf_op jit(solution)/shard_map/ppermute | solution.py:166
  15.0 8.5 %collective-permute-start.3 = (bf16[128,512]{1,0:T(8,128)(2,1)S(1)}, bf16[128,512]{1,0:T(8,128)(2,1)S(1)}, u32[]{:S(2)}, u32[]{:S(2)}) collective-permute-start(bf16[128,512]{1,0:T(8,128)(2,1)S(1)} %get-tuple-element.17.refs_4_), channel_id=1, source_target_pairs={{0,3},{1,2},{2,1},{3,0},{4,7},{5,6},{6,5},{7,4},{8,11},{9,10},{10,... | collective-permute-start | bytes 393224 | tf_op jit(solution)/shard_map/ppermute | solution.py:166
  23.9 1.7 %collective-permute-start.6 = (bf16[2,128,512]{2,1,0:T(8,128)(2,1)S(1)}, bf16[2,128,512]{2,1,0:T(8,128)(2,1)S(1)}, u32[]{:S(2)}, u32[]{:S(2)}) collective-permute-start(bf16[2,128,512]{2,1,0:T(8,128)(2,1)S(1)} %shard_map.72), channel_id=1, source_target_pairs={{0,4},{4,0},{8,12},{12,8},{16,20},{20,16},{24,28},{28,24},{1,5},{5... | collective-permute-start | bytes 786440 | tf_op jit(solution)/shard_map/ppermute | solution.py:166
  24.7 2.9 %copy-start.1 = (bf16[1024,512]{1,0:T(8,128)(2,1)S(1)}, bf16[1024,512]{1,0:T(8,128)(2,1)}, u32[]{:S(2)}) copy-start(bf16[1024,512]{1,0:T(8,128)(2,1)} %refs_4_.1) | copy-start | bytes 3145732
  24.7 7.2 %collective-permute-start.10 = (bf16[2,128,512]{2,1,0:T(8,128)(2,1)S(1)}, bf16[2,128,512]{2,1,0:T(8,128)(2,1)S(1)}, u32[]{:S(2)}, u32[]{:S(2)}) collective-permute-start(bf16[2,128,512]{2,1,0:T(8,128)(2,1)S(1)} %shard_map.76), channel_id=1, source_target_pairs={{0,4},{4,0},{8,12},{12,8},{16,20},{20,16},{24,28},{28,24},{1,5},{5... | collective-permute-start | bytes 786440 | tf_op jit(solution)/shard_map/ppermute | solution.py:166
  25.7 6.6 %collective-permute-start.12 = (bf16[128,512]{1,0:T(8,128)(2,1)S(1)}, bf16[128,512]{1,0:T(8,128)(2,1)S(1)}, u32[]{:S(2)}, u32[]{:S(2)}) collective-permute-start(bf16[128,512]{1,0:T(8,128)(2,1)S(1)} %fusion.4), channel_id=1, source_target_pairs={{0,8},{4,12},{8,0},{12,4},{16,24},{20,28},{24,16},{28,20},{1,9},{5... | collective-permute-start | bytes 393224 | tf_op jit(solution)/shard_map/ppermute | solution.py:166
  28.3 9.4 %copy-start.3 = (bf16[128,4096]{1,0:T(8,128)(2,1)S(1)}, bf16[128,4096]{1,0:T(8,128)(2,1)}, u32[]{:S(2)}) copy-start(bf16[128,4096]{1,0:T(8,128)(2,1)} %q_ref.3) | copy-start | bytes 3145732
  28.3 9.4 %copy-start.5 = (bf16[128,4096]{1,0:T(8,128)(2,1)S(1)}, bf16[128,4096]{1,0:T(8,128)(2,1)}, u32[]{:S(2)}) copy-start(bf16[128,4096]{1,0:T(8,128)(2,1)} %g_ref.3) | copy-start | bytes 3145732
  28.3 6.9 %collective-permute-start.7 = (bf16[128,512]{1,0:T(8,128)(2,1)S(1)}, bf16[128,512]{1,0:T(8,128)(2,1)S(1)}, u32[]{:S(2)}, u32[]{:S(2)}) collective-permute-start(bf16[128,512]{1,0:T(8,128)(2,1)S(1)} %get-tuple-element.19), channel_id=1, source_target_pairs={{0,1},{1,0},{2,3},{3,2},{4,5},{5,4},{6,7},{7,6},{8,9},{9,8},{10,11... | collective-permute-start | bytes 393224 | tf_op jit(solution)/shard_map/ppermute | solution.py:166
  29.9 7.8 %collective-permute-start.8 = (bf16[128,512]{1,0:T(8,128)(2,1)S(1)}, bf16[128,512]{1,0:T(8,128)(2,1)S(1)}, u32[]{:S(2)}, u32[]{:S(2)}) collective-permute-start(bf16[128,512]{1,0:T(8,128)(2,1)S(1)} %get-tuple-element.20), channel_id=1, source_target_pairs={{0,2},{1,3},{2,0},{3,1},{4,6},{5,7},{6,4},{7,5},{8,10},{9,11},{10,... | collective-permute-start | bytes 393224 | tf_op jit(solution)/shard_map/ppermute | solution.py:166
  31.4 6.3 %collective-permute-start.9 = (bf16[128,512]{1,0:T(8,128)(2,1)S(1)}, bf16[128,512]{1,0:T(8,128)(2,1)S(1)}, u32[]{:S(2)}, u32[]{:S(2)}) collective-permute-start(bf16[128,512]{1,0:T(8,128)(2,1)S(1)} %get-tuple-element.21), channel_id=1, source_target_pairs={{0,3},{1,2},{2,1},{3,0},{4,7},{5,6},{6,5},{7,4},{8,11},{9,10},{10,... | collective-permute-start | bytes 393224 | tf_op jit(solution)/shard_map/ppermute | solution.py:166
  32.0 7.6 %collective-permute-start.11 = (bf16[128,512]{1,0:T(8,128)(2,1)S(1)}, bf16[128,512]{1,0:T(8,128)(2,1)S(1)}, u32[]{:S(2)}, u32[]{:S(2)}) collective-permute-start(bf16[128,512]{1,0:T(8,128)(2,1)S(1)} %fusion.3), channel_id=1, source_target_pairs={{0,8},{4,12},{8,0},{12,4},{16,24},{20,28},{24,16},{28,20},{1,9},{5... | collective-permute-start | bytes 393224 | tf_op jit(solution)/shard_map/ppermute | solution.py:166
  32.3 7.3 %collective-permute-start.13 = (bf16[128,512]{1,0:T(8,128)(2,1)S(1)}, bf16[128,512]{1,0:T(8,128)(2,1)S(1)}, u32[]{:S(2)}, u32[]{:S(2)}) collective-permute-start(bf16[128,512]{1,0:T(8,128)(2,1)S(1)} %add_convert_fusion), channel_id=1, source_target_pairs={{0,16},{4,20},{8,24},{12,28},{16,0},{20,4},{24,8},{28,12},{1,17},{... | collective-permute-start | bytes 393224 | tf_op jit(solution)/shard_map/ppermute | solution.py:166

commit v5 on v4

--- a/solution.py
+++ b/solution.py
@@ -152,13 +152,16 @@
     return call(kernel, [struct(shape, dtype)], flops, (*blocks, *d_values, *after), in_specs)[0]
 
 
-def mark_kernel(*refs):
-    refs[-1][...] = jnp.zeros_like(refs[-1])
-
-
-def mark(arrays):
-    in_specs = [pl.BlockSpec(memory_space=pl.ANY)] * len(arrays)
-    return call(mark_kernel, [struct((8, 128), jnp.float32)], 100_000_000, arrays, in_specs)[0]
+def copy_kernel(n, *refs):
+    for source, out in zip(refs[:n], refs[-n:]):
+        out[...] = source[...]
+
+
+def copies_after(arrays, after):
+    n = len(arrays)
+    in_specs = [VMEM] * n + [pl.BlockSpec(memory_space=pl.ANY)] * len(after)
+    outs = [struct(array.shape, array.dtype) for array in arrays]
+    return call(functools.partial(copy_kernel, n), outs, 100_000_000, (*arrays, *after), in_specs)
 
 
 def swap(array, axis, distance):
@@ -189,17 +192,17 @@
     ordered = [blocks[k] for k in order], [all_d_values[k] for k in order]
     low, wide = jnp.bfloat16, jnp.float32
     halves = tuple(range(chips // 2, chips)), tuple(range(chips // 2))
-    tick = mark(blocks[1:])
+    parts = values_call([blocks[k] for k in order], value_matrix)
+    parts = [parts[order.index(k)] for k in range(nodes)]
     pairs, keeps = {}, ()
     for distances in halves:
-        send = weight_call(*ordered, 1, owners, distances, (tick, *keeps))
+        send = weight_call(*ordered, 1, owners, distances, (parts[0], *keeps))
         keep = weight_call(*ordered, 0, owners, distances, (), 500_000_000)
         keeps = (keep,)
         pair = keep + swap(send, "dp", 1).astype(wide)
         pairs.update((k, pair[i]) for i, k in enumerate(distances))
 
-    parts = values_call([blocks[k] for k in order], value_matrix, (pairs[chips // 2],))
-    parts = [parts[order.index(k)] for k in range(nodes)]
+    parts[1:] = copies_after(parts[1:], (pairs[chips // 2],))
     values = [parts[0]] + [swap(parts[k], "node", k) for k in range(1, nodes)]
     key_gradient = key_call(queries, attention_gradient, attention, values)
     owned = pairs[0]

time: 40.7 us -> 39.9 us (0.980)
  waiting for transfers between devices: 10.1 us -> 9.36 us
    ppermute x14, waiting for transfers between devices: 10.1 us -> 9.36 us  [swap(): return lax.ppermute(array, axis, [(i, i ^ distance) for i in range(size)])]
where the time goes in v5:
time: 39.9 us; the launch traced here: 39.7 us
  starting transfers between devices  18.2 us (46%)
  waiting for transfers between devices  9.36 us (23%)
  Pallas kernels  5.73 us (14%)
  local copies, waits for them, and re-layouts  4.71 us (12%)
  other arithmetic  0.93 us (2%)
  between operations  0.79 us (2%)
    ppermute x14, starting transfers between devices, swap(): return lax.ppermute(array, axis, [(i, i ^ distance) for i in range(size)])  18.2 us
    ppermute x14, waiting for transfers between devices, swap(): return lax.ppermute(array, axis, [(i, i ^ distance) for i in range(size)])  9.36 us
    pallas_call x9, Pallas kernels, call(): pl.pallas_call(kernel, in_specs=in_specs or [VMEM] * len(arguments), out_...  5.73 us
    unnamed x14, local copies, waits for them, and re-layouts  4.66 us
  transfers between devices with their start and end apart: 14, of which 6 were waited for; matrix products, arithmetic and copies ran while one was open for 1% of the time, Pallas kernels for 13%

profile of v5, /device:TPU:0, one launch (start us, length us, event | category | flops | bytes accessed | tf_op | source)
XLA Modules:
  0.0 39.7 jit_solution(2676608866926570419)
XLA Ops:
  0.6 1.2 %copy-done = bf16[128,4096]{1,0:T(8,128)(2,1)S(1)} copy-done((bf16[128,4096]{1,0:T(8,128)(2,1)S(1)}, bf16[128,4096]{1,0:T(8,128)(2,1)}, u32[]{:S(2)}) %copy-start) | copy-done | bytes 1048600
  2.0 4.0 %collective-permute-start = (bf16[128,1024]{1,0:T(8,128)(2,1)S(1)}, bf16[128,1024]{1,0:T(8,128)(2,1)S(1)}, u32[]{:S(2)}, u32[]{:S(2)}) collective-permute-start(bf16[128,1024]{1,0:T(8,128)(2,1)S(1)} %get-tuple-element.17), channel_id=1, source_target_pairs={{0,3},{1,2},{2,1},{3,0},{4,7},{5,6},{6,5},{7,4},{8,11},{9,10},{10,... | collective-permute-start | bytes 786440 | tf_op jit(solution)/shard_map/ppermute | solution.py:169
  5.9 0.5 %collective-permute-start.1 = (bf16[128,1024]{1,0:T(8,128)(2,1)S(1)}, bf16[128,1024]{1,0:T(8,128)(2,1)S(1)}, u32[]{:S(2)}, u32[]{:S(2)}) collective-permute-start(bf16[128,1024]{1,0:T(8,128)(2,1)S(1)} %get-tuple-element.18), channel_id=1, source_target_pairs={{0,2},{1,3},{2,0},{3,1},{4,6},{5,7},{6,4},{7,5},{8,10},{9,11},{10,... | collective-permute-start | bytes 786440 | tf_op jit(solution)/shard_map/ppermute | solution.py:169
  6.6 1.3 %copy-done.2 = bf16[128,4096]{1,0:T(8,128)(2,1)S(1)} copy-done((bf16[128,4096]{1,0:T(8,128)(2,1)S(1)}, bf16[128,4096]{1,0:T(8,128)(2,1)}, u32[]{:S(2)}) %copy-start.2) | copy-done | bytes 1048600
  7.9 1.2 %copy-done.4 = bf16[128,4096]{1,0:T(8,128)(2,1)S(1)} copy-done((bf16[128,4096]{1,0:T(8,128)(2,1)S(1)}, bf16[128,4096]{1,0:T(8,128)(2,1)}, u32[]{:S(2)}) %copy-start.4) | copy-done | bytes 1048600
  9.1 0.9 %copy-done.6 = bf16[128,512]{1,0:T(8,128)(2,1)S(1)} copy-done((bf16[128,512]{1,0:T(8,128)(2,1)S(1)}, bf16[128,512]{1,0:T(8,128)(2,1)}, u32[]{:S(2)}) %copy-start.6) | copy-done | bytes 131096
  10.0 1.6 %shard_map.68 = (bf16[128,512]{1,0:T(8,128)(2,1)S(1)}, f32[128,4096]{1,0:T(8,128)S(1)}) custom-call(bf16[128,4096]{1,0:T(8,128)(2,1)S(1)} %copy-done.2, bf16[128,512]{1,0:T(8,128)(2,1)S(1)} %copy-done.6, bf16[128,4096]{1,0:T(8,128)(2,1)S(1)} %copy-done.4), custom_call_target="tpu_custom_call" | custom-call | flops 3000000000 | bytes 1000000 | tf_op jit(solution)/shard_map/pallas_call | solution.py:40
  11.6 1.9 %collective-permute-start.5 = (bf16[128,512]{1,0:T(8,128)(2,1)S(1)}, bf16[128,512]{1,0:T(8,128)(2,1)S(1)}, u32[]{:S(2)}, u32[]{:S(2)}) collective-permute-start(bf16[128,512]{1,0:T(8,128)(2,1)S(1)} %get-tuple-element.24.refs_4_), channel_id=1, source_target_pairs={{0,1},{1,0},{2,3},{3,2},{4,5},{5,4},{6,7},{7,6},{8,9},{9,8},{10,11... | collective-permute-start | bytes 393224 | tf_op jit(solution)/shard_map/ppermute | solution.py:169
  13.5 1.5 %collective-permute-start.4 = (bf16[128,512]{1,0:T(8,128)(2,1)S(1)}, bf16[128,512]{1,0:T(8,128)(2,1)S(1)}, u32[]{:S(2)}, u32[]{:S(2)}) collective-permute-start(bf16[128,512]{1,0:T(8,128)(2,1)S(1)} %get-tuple-element.24.refs_4_), channel_id=1, source_target_pairs={{0,2},{1,3},{2,0},{3,1},{4,6},{5,7},{6,4},{7,5},{8,10},{9,11},{10,... | collective-permute-start | bytes 393224 | tf_op jit(solution)/shard_map/ppermute | solution.py:169
  15.0 1.0 %collective-permute-start.3 = (bf16[128,512]{1,0:T(8,128)(2,1)S(1)}, bf16[128,512]{1,0:T(8,128)(2,1)S(1)}, u32[]{:S(2)}, u32[]{:S(2)}) collective-permute-start(bf16[128,512]{1,0:T(8,128)(2,1)S(1)} %get-tuple-element.24.refs_4_), channel_id=1, source_target_pairs={{0,3},{1,2},{2,1},{3,0},{4,7},{5,6},{6,5},{7,4},{8,11},{9,10},{10,... | collective-permute-start | bytes 393224 | tf_op jit(solution)/shard_map/ppermute | solution.py:169
  16.0 1.9 %collective-permute-done.1.refs_2_ = bf16[128,1024]{1,0:T(8,128)(2,1)S(1)} collective-permute-done((bf16[128,1024]{1,0:T(8,128)(2,1)S(1)}, bf16[128,1024]{1,0:T(8,128)(2,1)S(1)}, u32[]{:S(2)}, u32[]{:S(2)}) %collective-permute-start.1) | collective-permute-done | bytes 262176 | tf_op jit(solution)/shard_map/ppermute | solution.py:169
  18.0 1.3 %collective-permute-done.2.refs_3_ = bf16[128,1024]{1,0:T(8,128)(2,1)S(1)} collective-permute-done((bf16[128,1024]{1,0:T(8,128)(2,1)S(1)}, bf16[128,1024]{1,0:T(8,128)(2,1)S(1)}, u32[]{:S(2)}, u32[]{:S(2)}) %collective-permute-start.2) | collective-permute-done | bytes 262176 | tf_op jit(solution)/shard_map/ppermute | solution.py:169
  19.3 0.7 %shard_map.70 = (f32[128,512]{1,0:T(8,128)S(1)}, bf16[128,512]{1,0:T(8,128)(2,1)S(1)}, bf16[128,512]{1,0:T(8,128)(2,1)S(1)}, bf16[128,512]{1,0:T(8,128)(2,1)S(1)}) custom-call(bf16[128,1024]{1,0:T(8,128)(2,1)S(1)} %get-tuple-element.16.refs_0_, bf16[128,1024]{1,0:T(8,128)(2,1)S(1)} %collective-permute-done.refs_1_, ...), custom_call_target="tpu_custom_call" | custom-call | flops 1500000000 | bytes 1000000 | tf_op jit(solution)/shard_map/pallas_call | solution.py:40
  20.0 2.1 %collective-permute-done.5.refs_7_ = bf16[128,512]{1,0:T(8,128)(2,1)S(1)} collective-permute-done((bf16[128,512]{1,0:T(8,128)(2,1)S(1)}, bf16[128,512]{1,0:T(8,128)(2,1)S(1)}, u32[]{:S(2)}, u32[]{:S(2)}) %collective-permute-start.5) | collective-permute-done | bytes 131104 | tf_op jit(solution)/shard_map/ppermute | solution.py:169
  22.1 1.4 %collective-permute-done.3.refs_5_ = bf16[128,512]{1,0:T(8,128)(2,1)S(1)} collective-permute-done((bf16[128,512]{1,0:T(8,128)(2,1)S(1)}, bf16[128,512]{1,0:T(8,128)(2,1)S(1)}, u32[]{:S(2)}, u32[]{:S(2)}) %collective-permute-start.3) | collective-permute-done | bytes 131104 | tf_op jit(solution)/shard_map/ppermute | solution.py:169
  24.7 0.6 %collective-permute-start.10 = (bf16[2,128,512]{2,1,0:T(8,128)(2,1)S(1)}, bf16[2,128,512]{2,1,0:T(8,128)(2,1)S(1)}, u32[]{:S(2)}, u32[]{:S(2)}) collective-permute-start(bf16[2,128,512]{2,1,0:T(8,128)(2,1)S(1)} %shard_map.76), channel_id=1, source_target_pairs={{0,4},{4,0},{8,12},{12,8},{16,20},{20,16},{24,28},{28,24},{1,5},{5... | collective-permute-start | bytes 786440 | tf_op jit(solution)/shard_map/ppermute | solution.py:169
  25.7 1.8 %collective-permute-start.12 = (bf16[128,512]{1,0:T(8,128)(2,1)S(1)}, bf16[128,512]{1,0:T(8,128)(2,1)S(1)}, u32[]{:S(2)}, u32[]{:S(2)}) collective-permute-start(bf16[128,512]{1,0:T(8,128)(2,1)S(1)} %fusion.4), channel_id=1, source_target_pairs={{0,8},{4,12},{8,0},{12,4},{16,24},{20,28},{24,16},{28,20},{1,9},{5... | collective-permute-start | bytes 393224 | tf_op jit(solution)/shard_map/ppermute | solution.py:169
  27.6 1.6 %collective-permute-start.7 = (bf16[128,512]{1,0:T(8,128)(2,1)S(1)}, bf16[128,512]{1,0:T(8,128)(2,1)S(1)}, u32[]{:S(2)}, u32[]{:S(2)}) collective-permute-start(bf16[128,512]{1,0:T(8,128)(2,1)S(1)} %get-tuple-element.25), channel_id=1, source_target_pairs={{0,1},{1,0},{2,3},{3,2},{4,5},{5,4},{6,7},{7,6},{8,9},{9,8},{10,11... | collective-permute-start | bytes 393224 | tf_op jit(solution)/shard_map/ppermute | solution.py:169
  29.2 1.5 %collective-permute-start.8 = (bf16[128,512]{1,0:T(8,128)(2,1)S(1)}, bf16[128,512]{1,0:T(8,128)(2,1)S(1)}, u32[]{:S(2)}, u32[]{:S(2)}) collective-permute-start(bf16[128,512]{1,0:T(8,128)(2,1)S(1)} %get-tuple-element.26), channel_id=1, source_target_pairs={{0,2},{1,3},{2,0},{3,1},{4,6},{5,7},{6,4},{7,5},{8,10},{9,11},{10,... | collective-permute-start | bytes 393224 | tf_op jit(solution)/shard_map/ppermute | solution.py:169
  30.7 0.5 %collective-permute-start.9 = (bf16[128,512]{1,0:T(8,128)(2,1)S(1)}, bf16[128,512]{1,0:T(8,128)(2,1)S(1)}, u32[]{:S(2)}, u32[]{:S(2)}) collective-permute-start(bf16[128,512]{1,0:T(8,128)(2,1)S(1)} %get-tuple-element.27), channel_id=1, source_target_pairs={{0,3},{1,2},{2,1},{3,0},{4,7},{5,6},{6,5},{7,4},{8,11},{9,10},{10,... | collective-permute-start | bytes 393224 | tf_op jit(solution)/shard_map/ppermute | solution.py:169
  31.6 2.8 %collective-permute-start.13 = (bf16[128,512]{1,0:T(8,128)(2,1)S(1)}, bf16[128,512]{1,0:T(8,128)(2,1)S(1)}, u32[]{:S(2)}, u32[]{:S(2)}) collective-permute-start(bf16[128,512]{1,0:T(8,128)(2,1)S(1)} %add_convert_fusion), channel_id=1, source_target_pairs={{0,16},{4,20},{8,24},{12,28},{16,0},{20,4},{24,8},{28,12},{1,17},{... | collective-permute-start | bytes 393224 | tf_op jit(solution)/shard_map/ppermute | solution.py:169
  34.5 2.5 %collective-permute-done.8.rest_2_ = bf16[128,512]{1,0:T(8,128)(2,1)S(1)} collective-permute-done((bf16[128,512]{1,0:T(8,128)(2,1)S(1)}, bf16[128,512]{1,0:T(8,128)(2,1)S(1)}, u32[]{:S(2)}, u32[]{:S(2)}) %collective-permute-start.8) | collective-permute-done | bytes 131104 | tf_op jit(solution)/shard_map/ppermute | solution.py:169
  36.9 1.9 %shard_map.74 = bf16[128,512]{1,0:T(8,128)(2,1)} custom-call(bf16[128,4096]{1,0:T(8,128)(2,1)S(1)} %copy-done.3, bf16[128,4096]{1,0:T(8,128)(2,1)S(1)} %copy-done.5, f32[128,4096]{1,0:T(8,128)S(1)} %get-tuple-element.15.p_ref, f32[128,512]{1,0:T(8,128)S(1)} %get-tuple-element.20.refs_8_.rest_0_, bf16[128,512]{1,0:T(8,128)(2,1)S(1)} %collective-permute-done.7.rest_1_, ...), custom_call_target="tpu_custom_call" | custom-call | flops 2500000000 | bytes 1000000 | tf_op jit(solution)/shard_map/pallas_call | solution.py:40
  39.0 0.8 %fusion.2 = f32[128,512]{1,0:T(8,128)} fusion(f32[2,128,512]{2,1,0:T(8,128)S(1)} %convert_add_fusion, bf16[128,512]{1,0:T(8,128)(2,1)S(1)} %collective-permute-done.13, bf16[128,512]{1,0:T(8,128)(2,1)S(1)} %collective-permute-done.11), kind=kLoop, calls=%fused_computation.7 | loop fusion | flops 327680 | bytes 786432 | tf_op jit(solution)/shard_map/div | solution.py:216
  (34 shorter events, 2.4 us)
Async XLA Ops:
  0.6 1.2 %copy-start = (bf16[128,4096]{1,0:T(8,128)(2,1)S(1)}, bf16[128,4096]{1,0:T(8,128)(2,1)}, u32[]{:S(2)}) copy-start(bf16[128,4096]{1,0:T(8,128)(2,1)} %source_ref.1) | copy-start | bytes 3145732
  2.0 13.0 %collective-permute-start = (bf16[128,1024]{1,0:T(8,128)(2,1)S(1)}, bf16[128,1024]{1,0:T(8,128)(2,1)S(1)}, u32[]{:S(2)}, u32[]{:S(2)}) collective-permute-start(bf16[128,1024]{1,0:T(8,128)(2,1)S(1)} %get-tuple-element.17), channel_id=1, source_target_pairs={{0,3},{1,2},{2,1},{3,0},{4,7},{5,6},{6,5},{7,4},{8,11},{9,10},{10,... | collective-permute-start | bytes 786440 | tf_op jit(solution)/shard_map/ppermute | solution.py:169
  5.9 12.0 %collective-permute-start.1 = (bf16[128,1024]{1,0:T(8,128)(2,1)S(1)}, bf16[128,1024]{1,0:T(8,128)(2,1)S(1)}, u32[]{:S(2)}, u32[]{:S(2)}) collective-permute-start(bf16[128,1024]{1,0:T(8,128)(2,1)S(1)} %get-tuple-element.18), channel_id=1, source_target_pairs={{0,2},{1,3},{2,0},{3,1},{4,6},{5,7},{6,4},{7,5},{8,10},{9,11},{10,... | collective-permute-start | bytes 786440 | tf_op jit(solution)/shard_map/ppermute | solution.py:169
  6.4 12.9 %copy-start.1 = (bf16[1024,512]{1,0:T(8,128)(2,1)S(1)}, bf16[1024,512]{1,0:T(8,128)(2,1)}, u32[]{:S(2)}) copy-start(bf16[1024,512]{1,0:T(8,128)(2,1)} %refs_4_.1) | copy-start | bytes 3145732
  6.4 12.9 %collective-permute-start.2 = (bf16[128,1024]{1,0:T(8,128)(2,1)S(1)}, bf16[128,1024]{1,0:T(8,128)(2,1)S(1)}, u32[]{:S(2)}, u32[]{:S(2)}) collective-permute-start(bf16[128,1024]{1,0:T(8,128)(2,1)S(1)} %get-tuple-element.19), channel_id=1, source_target_pairs={{0,1},{1,0},{2,3},{3,2},{4,5},{5,4},{6,7},{7,6},{8,9},{9,8},{10,11... | collective-permute-start | bytes 786440 | tf_op jit(solution)/shard_map/ppermute | solution.py:169
  6.6 1.3 %copy-start.2 = (bf16[128,4096]{1,0:T(8,128)(2,1)S(1)}, bf16[128,4096]{1,0:T(8,128)(2,1)}, u32[]{:S(2)}) copy-start(bf16[128,4096]{1,0:T(8,128)(2,1)} %q_ref.3) | copy-start | bytes 3145732
  7.9 1.2 %copy-start.4 = (bf16[128,4096]{1,0:T(8,128)(2,1)S(1)}, bf16[128,4096]{1,0:T(8,128)(2,1)}, u32[]{:S(2)}) copy-start(bf16[128,4096]{1,0:T(8,128)(2,1)} %g_ref.3) | copy-start | bytes 3145732
  9.1 0.9 %copy-start.6 = (bf16[128,512]{1,0:T(8,128)(2,1)S(1)}, bf16[128,512]{1,0:T(8,128)(2,1)}, u32[]{:S(2)}) copy-start(bf16[128,512]{1,0:T(8,128)(2,1)} %k_ref.1) | copy-start | bytes 393220
  11.6 10.5 %collective-permute-start.5 = (bf16[128,512]{1,0:T(8,128)(2,1)S(1)}, bf16[128,512]{1,0:T(8,128)(2,1)S(1)}, u32[]{:S(2)}, u32[]{:S(2)}) collective-permute-start(bf16[128,512]{1,0:T(8,128)(2,1)S(1)} %get-tuple-element.24.refs_4_), channel_id=1, source_target_pairs={{0,1},{1,0},{2,3},{3,2},{4,5},{5,4},{6,7},{7,6},{8,9},{9,8},{10,11... | collective-permute-start | bytes 393224 | tf_op jit(solution)/shard_map/ppermute | solution.py:169
  13.5 8.6 %collective-permute-start.4 = (bf16[128,512]{1,0:T(8,128)(2,1)S(1)}, bf16[128,512]{1,0:T(8,128)(2,1)S(1)}, u32[]{:S(2)}, u32[]{:S(2)}) collective-permute-start(bf16[128,512]{1,0:T(8,128)(2,1)S(1)} %get-tuple-element.24.refs_4_), channel_id=1, source_target_pairs={{0,2},{1,3},{2,0},{3,1},{4,6},{5,7},{6,4},{7,5},{8,10},{9,11},{10,... | collective-permute-start | bytes 393224 | tf_op jit(solution)/shard_map/ppermute | solution.py:169
  15.0 8.5 %collective-permute-start.3 = (bf16[128,512]{1,0:T(8,128)(2,1)S(1)}, bf16[128,512]{1,0:T(8,128)(2,1)S(1)}, u32[]{:S(2)}, u32[]{:S(2)}) collective-permute-start(bf16[128,512]{1,0:T(8,128)(2,1)S(1)} %get-tuple-element.24.refs_4_), channel_id=1, source_target_pairs={{0,3},{1,2},{2,1},{3,0},{4,7},{5,6},{6,5},{7,4},{8,11},{9,10},{10,... | collective-permute-start | bytes 393224 | tf_op jit(solution)/shard_map/ppermute | solution.py:169
  23.9 1.7 %collective-permute-start.6 = (bf16[2,128,512]{2,1,0:T(8,128)(2,1)S(1)}, bf16[2,128,512]{2,1,0:T(8,128)(2,1)S(1)}, u32[]{:S(2)}, u32[]{:S(2)}) collective-permute-start(bf16[2,128,512]{2,1,0:T(8,128)(2,1)S(1)} %shard_map.72), channel_id=1, source_target_pairs={{0,4},{4,0},{8,12},{12,8},{16,20},{20,16},{24,28},{28,24},{1,5},{5... | collective-permute-start | bytes 786440 | tf_op jit(solution)/shard_map/ppermute | solution.py:169
  24.7 6.5 %collective-permute-start.10 = (bf16[2,128,512]{2,1,0:T(8,128)(2,1)S(1)}, bf16[2,128,512]{2,1,0:T(8,128)(2,1)S(1)}, u32[]{:S(2)}, u32[]{:S(2)}) collective-permute-start(bf16[2,128,512]{2,1,0:T(8,128)(2,1)S(1)} %shard_map.76), channel_id=1, source_target_pairs={{0,4},{4,0},{8,12},{12,8},{16,20},{20,16},{24,28},{28,24},{1,5},{5... | collective-permute-start | bytes 786440 | tf_op jit(solution)/shard_map/ppermute | solution.py:169
  25.7 11.3 %copy-start.3 = (bf16[128,4096]{1,0:T(8,128)(2,1)S(1)}, bf16[128,4096]{1,0:T(8,128)(2,1)}, u32[]{:S(2)}) copy-start(bf16[128,4096]{1,0:T(8,128)(2,1)} %q_ref.3) | copy-start | bytes 3145732
  25.7 11.3 %copy-start.5 = (bf16[128,4096]{1,0:T(8,128)(2,1)S(1)}, bf16[128,4096]{1,0:T(8,128)(2,1)}, u32[]{:S(2)}) copy-start(bf16[128,4096]{1,0:T(8,128)(2,1)} %g_ref.3) | copy-start | bytes 3145732
  25.7 5.9 %collective-permute-start.12 = (bf16[128,512]{1,0:T(8,128)(2,1)S(1)}, bf16[128,512]{1,0:T(8,128)(2,1)S(1)}, u32[]{:S(2)}, u32[]{:S(2)}) collective-permute-start(bf16[128,512]{1,0:T(8,128)(2,1)S(1)} %fusion.4), channel_id=1, source_target_pairs={{0,8},{4,12},{8,0},{12,4},{16,24},{20,28},{24,16},{28,20},{1,9},{5... | collective-permute-start | bytes 393224 | tf_op jit(solution)/shard_map/ppermute | solution.py:169
  27.6 6.9 %collective-permute-start.7 = (bf16[128,512]{1,0:T(8,128)(2,1)S(1)}, bf16[128,512]{1,0:T(8,128)(2,1)S(1)}, u32[]{:S(2)}, u32[]{:S(2)}) collective-permute-start(bf16[128,512]{1,0:T(8,128)(2,1)S(1)} %get-tuple-element.25), channel_id=1, source_target_pairs={{0,1},{1,0},{2,3},{3,2},{4,5},{5,4},{6,7},{7,6},{8,9},{9,8},{10,11... | collective-permute-start | bytes 393224 | tf_op jit(solution)/shard_map/ppermute | solution.py:169
  29.2 7.8 %collective-permute-start.8 = (bf16[128,512]{1,0:T(8,128)(2,1)S(1)}, bf16[128,512]{1,0:T(8,128)(2,1)S(1)}, u32[]{:S(2)}, u32[]{:S(2)}) collective-permute-start(bf16[128,512]{1,0:T(8,128)(2,1)S(1)} %get-tuple-element.26), channel_id=1, source_target_pairs={{0,2},{1,3},{2,0},{3,1},{4,6},{5,7},{6,4},{7,5},{8,10},{9,11},{10,... | collective-permute-start | bytes 393224 | tf_op jit(solution)/shard_map/ppermute | solution.py:169
  30.7 6.3 %collective-permute-start.9 = (bf16[128,512]{1,0:T(8,128)(2,1)S(1)}, bf16[128,512]{1,0:T(8,128)(2,1)S(1)}, u32[]{:S(2)}, u32[]{:S(2)}) collective-permute-start(bf16[128,512]{1,0:T(8,128)(2,1)S(1)} %get-tuple-element.27), channel_id=1, source_target_pairs={{0,3},{1,2},{2,1},{3,0},{4,7},{5,6},{6,5},{7,4},{8,11},{9,10},{10,... | collective-permute-start | bytes 393224 | tf_op jit(solution)/shard_map/ppermute | solution.py:169
  31.3 7.6 %collective-permute-start.11 = (bf16[128,512]{1,0:T(8,128)(2,1)S(1)}, bf16[128,512]{1,0:T(8,128)(2,1)S(1)}, u32[]{:S(2)}, u32[]{:S(2)}) collective-permute-start(bf16[128,512]{1,0:T(8,128)(2,1)S(1)} %fusion.3), channel_id=1, source_target_pairs={{0,8},{4,12},{8,0},{12,4},{16,24},{20,28},{24,16},{28,20},{1,9},{5... | collective-permute-start | bytes 393224 | tf_op jit(solution)/shard_map/ppermute | solution.py:169
  31.6 7.3 %collective-permute-start.13 = (bf16[128,512]{1,0:T(8,128)(2,1)S(1)}, bf16[128,512]{1,0:T(8,128)(2,1)S(1)}, u32[]{:S(2)}, u32[]{:S(2)}) collective-permute-start(bf16[128,512]{1,0:T(8,128)(2,1)S(1)} %add_convert_fusion), channel_id=1, source_target_pairs={{0,16},{4,20},{8,24},{12,28},{16,0},{20,4},{24,8},{28,12},{1,17},{... | collective-permute-start | bytes 393224 | tf_op jit(solution)/shard_map/ppermute | solution.py:169
